TPU v7x, 32 devices: a whole 2x2x4 slice. The times are simulated.
32 devices in a mesh: groups: 2 (over y), morton: 4 (over z), chan: 4 (over x, core).
Axes of the slice: x: 2, y: 2, z: 4, core: 2. Of those that a mesh axis runs over, the one named last changes fastest.
Arguments:
- parents: bfloat16 [16, 256, 512], P(('groups', 'morton'), 'chan'), parts along dimension 0, may hold values from -6 to 6
- up_weight: bfloat16 [8, 256, 128], replicated, may hold values from -0.375 to 0.375
- conv_weight: bfloat16 [27, 128, 128], replicated, may hold values from -0.1875 to 0.1875
- conv_bias: float32 [128], replicated, may hold values from -3 to 3
- child_dest: int32 [128], P(('groups', 'morton')), parts along dimension 0, may hold values from -1 to 31, as said below
- face_nbr: int32 [64, 6], P(('groups', 'morton')), parts along dimension 0, may hold values from -1 to 31, as said below
Outputs:
- children_out: bfloat16 [64, 128, 512], P(('groups', 'morton', 'chan')), parts along dimension 0
There are 2 independent parts, one for each index of `groups`. A program takes and returns all parts, laid end to end along the dimension named above; an argument that names none is the same for every part. Nothing has to cross between parts.
Inputs may be any that keep to these rules, and one draw needn't show every extreme that they name: `child_dest`: candidates are numbered parent-major, octant minor. Kept candidates have positions rising with their number, every position from 0 to 31 is taken once, and the kept children of the parents of one Morton range lie no more than 2 positions outside that range's own 8 positions; in every draw some range passes exactly 2 to the next range and some range exactly 2 to the previous one. `face_nbr`: column k names the kept block across face k (low x, high x, low y, high y, low z, high z) in the window's block grid, or -1 where there is none. Where a range's rows already hold 4 entries naming one other range, its later such entries are also -1 and are treated as empty. The entries of the rows of one Morton range (its 8 positions) that name blocks of one other range number at most 4.
All inputs are finite; a program needn't handle non-finite values.
Results may differ from a plain program's by a relative error of at most 0.0049.
Values may be sent and summed in bfloat16 or wider, within the bound.
A program may use at most 64 MiB of HBM per device.

v0:
```python
import jax
import jax.numpy as jnp
from jax import lax
from jax.sharding import PartitionSpec as P

MOVE_CAP = 2


OPPOSITE = (1, 0, 3, 2, 5, 4)


def passed_along(block, axis, distance):
    devices = range(lax.axis_size(axis))
    route = [(i - distance, i) for i in devices if i - distance in devices]
    return lax.ppermute(block, axis, route)


def spread_children(spread):
    block_total = spread.shape[0]
    channels = spread.shape[2]
    grid = spread.reshape(block_total, 2, 2, 2, channels, 8, 8, 8)
    grid = grid.transpose(0, 4, 5, 1, 6, 2, 7, 3).reshape(block_total, channels, 2, 8, 2, 8, 2, 8)
    grid = grid.transpose(0, 6, 4, 2, 1, 3, 5, 7)
    return grid.reshape(block_total * 8, channels, 512)


def face_slabs(blocks):
    block_total = blocks.shape[0]
    channels = blocks.shape[1]
    padded_cube = blocks.reshape(block_total, channels, 8, 8, 8)
    layers = [
        padded_cube[:, :, 0],
        padded_cube[:, :, 7],
        padded_cube[:, :, :, 0],
        padded_cube[:, :, :, 7],
        padded_cube[:, :, :, :, 0],
        padded_cube[:, :, :, :, 7],
    ]
    return jnp.stack([layer.reshape(block_total, channels, 64) for layer in layers], axis=1)


def convolve(blocks, beside, conv_weight, conv_bias):
    block_total = blocks.shape[0]
    channels = blocks.shape[1]
    padded_cube = jnp.pad(
        blocks.reshape(block_total, channels, 8, 8, 8), ((0, 0), (0, 0), (1, 1), (1, 1), (1, 1))
    )
    side_faces = beside.reshape(block_total, channels, 6, 8, 8)
    padded_cube = padded_cube.at[:, :, 0, 1:9, 1:9].set(side_faces[:, :, 0])
    padded_cube = padded_cube.at[:, :, 9, 1:9, 1:9].set(side_faces[:, :, 1])
    padded_cube = padded_cube.at[:, :, 1:9, 0, 1:9].set(side_faces[:, :, 2])
    padded_cube = padded_cube.at[:, :, 1:9, 9, 1:9].set(side_faces[:, :, 3])
    padded_cube = padded_cube.at[:, :, 1:9, 1:9, 0].set(side_faces[:, :, 4])
    padded_cube = padded_cube.at[:, :, 1:9, 1:9, 9].set(side_faces[:, :, 5])
    running = jnp.zeros((block_total, conv_weight.shape[2], 512), jnp.float32)
    for shift_x in range(3):
        for shift_y in range(3):
            for shift_z in range(3):
                tap_view = padded_cube[
                    :, :, shift_x : shift_x + 8, shift_y : shift_y + 8, shift_z : shift_z + 8
                ].reshape(block_total, channels, 512)
                weight_tap = conv_weight[9 * shift_x + 3 * shift_y + shift_z]
                running = running + jnp.einsum(
                    "cd,bcv->bdv", weight_tap, tap_view, preferred_element_type=jnp.float32
                )
    return jax.nn.silu(running + conv_bias[None, :, None]).astype(jnp.bfloat16)


def per_device(parents, up_weight, conv_weight, conv_bias, child_dest, face_nbr):
    own_depth = up_weight.shape[2] // lax.axis_size("chan")
    own_weight = lax.dynamic_slice_in_dim(
        up_weight, lax.axis_index("chan") * own_depth, own_depth, 2
    )
    spread = jnp.einsum(
        "ocd,pcv->podv",
        own_weight,
        lax.all_gather(parents, "chan", axis=1, tiled=True),
        preferred_element_type=jnp.float32,
    )
    candidates = spread_children(spread).astype(jnp.bfloat16)
    cand_count = candidates.shape[0]
    flat_rows = candidates.reshape(cand_count, own_depth * 512)
    block_count = face_nbr.shape[0]
    capacity = MOVE_CAP
    owner_id = lax.axis_index("morton")
    is_kept = child_dest >= 0
    owner_dev = jnp.where(is_kept, child_dest // block_count, -5)
    position = child_dest % block_count
    row_ids = jnp.arange(block_count, dtype=jnp.int32)[:, None]
    slot_ids = jnp.arange(capacity, dtype=jnp.int32)[:, None]
    local_map = ((owner_dev == owner_id)[None, :] & (position[None, :] == row_ids)).astype(
        jnp.bfloat16
    )
    up_map = ((owner_dev == owner_id + 1)[None, :] & (position[None, :] == slot_ids)).astype(
        jnp.bfloat16
    )
    down_map = (
        (owner_dev == owner_id - 1)[None, :]
        & (position[None, :] == slot_ids + block_count - capacity)
    ).astype(jnp.bfloat16)
    settled = jnp.dot(local_map, flat_rows, preferred_element_type=jnp.float32)
    packed = jnp.stack(
        [
            jnp.dot(up_map, flat_rows, preferred_element_type=jnp.float32),
            jnp.dot(down_map, flat_rows, preferred_element_type=jnp.float32),
        ]
    ).astype(jnp.bfloat16)
    arrived = []
    for which_side, offset_by in ((0, 1), (1, -1)):
        arrived.append(passed_along(packed[which_side], "morton", offset_by))
    settled = settled + jnp.pad(
        arrived[0].astype(jnp.float32), ((0, block_count - capacity), (0, 0))
    )
    settled = settled + jnp.pad(
        arrived[1].astype(jnp.float32), ((block_count - capacity, 0), (0, 0))
    )
    blocks = settled.astype(jnp.bfloat16).reshape(block_count, own_depth, 512)
    layers = face_slabs(lax.all_gather(blocks, "morton", axis=0, tiled=True))
    part_count = layers.shape[0]
    hits = (face_nbr[:, :, None] == jnp.arange(part_count, dtype=jnp.int32)[None, None, :]).astype(
        jnp.bfloat16
    )
    flipped = jnp.stack([layers[:, slab_index] for slab_index in OPPOSITE], axis=1).reshape(
        part_count, 6, own_depth * 64
    )
    gathered = jnp.einsum("ikj,jkx->kix", hits, flipped, preferred_element_type=jnp.float32)
    beside = (
        gathered.astype(jnp.bfloat16)
        .reshape(6, block_count, own_depth, 64)
        .transpose(1, 2, 0, 3)
        .reshape(block_count, own_depth, 384)
    )
    moved_blocks, moved_faces = (
        lax.all_to_all(blocks, "chan", split_axis=0, concat_axis=1, tiled=True),
        lax.all_to_all(beside, "chan", split_axis=0, concat_axis=1, tiled=True),
    )
    return convolve(moved_blocks, moved_faces, conv_weight, conv_bias)


def solution(mesh):
    placed = (
        P(("groups", "morton"), "chan", None),
        P(),
        P(),
        P(),
        P(("groups", "morton")),
        P(("groups", "morton"), None),
    )
    return jax.shard_map(
        per_device,
        mesh=mesh,
        in_specs=placed,
        out_specs=P(("groups", "morton", "chan"), None, None),
        check_vma=False,
    )
```

profile of v0, /device:TPU:0, one launch (start us, length us, event | category | flops | bytes accessed | tf_op | source)
XLA Modules:
  0.0 156.4 jit_solution(8326639940054983092)
XLA Ops:
  6.5 8.9 %all_gather.6 = bf16[2,256,512]{2,1,0:T(8,128)(2,1)S(1)} all-gather(bf16[2,64,512]{2,1,0:T(8,128)(2,1)} %param.18), channel_id=1, replica_groups=mesh['groups'=2,'morton'=4,'chan'=4] {'chan'}, dimensions={1}, use_global_device_ids=true | all-gather | bytes 655360 | tf_op jit(solution)/shard_map/all_gather | solution.py:77
  15.5 0.6 fusion.11
  16.1 1.7 %copy.75 = bf16[2,8,32,512]{2,3,1,0:T(8,128)(2,1)} copy(bf16[2,8,32,512]{3,2,0,1:T(8,128)(2,1)S(1)} %fusion.11) | data formatting | bytes 1048576 | tf_op jit(solution)/shard_map/ocd,pcv->podv/transpose | solution.py:74
  17.8 5.0 %copy.76 = bf16[2,32,8,2,8,2,8,2]{1,7,6,5,4,3,2,0:T(2,128)(2,1)S(1)} copy(bf16[2,32,8,2,8,2,8,2]{1,6,4,2,7,5,3,0:T(8,128)(2,1)} %bitcast.267) | data formatting | bytes 1048576 | tf_op jit(solution)/shard_map/convert_element_type | solution.py:80
  22.8 13.6 %copy.77 = bf16[2,2,2,2,32,8,8,8]{7,6,5,4,3,2,1,0:T(8,128)(2,1)} copy(bf16[2,2,2,2,32,8,8,8]{4,7,1,6,2,5,3,0:T(8,128)(2,1)S(1)} %bitcast.266) | data formatting | bytes 1048576 | tf_op jit(solution)/shard_map/convert_element_type | solution.py:80
  36.5 18.7 %convert_element_type.39 = bf16[16,16384]{1,0:T(8,128)(2,1)S(1)} reshape(bf16[2,2,2,2,32,8,8,8]{7,6,5,4,3,2,1,0:T(8,128)(2,1)} %copy.77) | data formatting | bytes 1048576 | tf_op jit(solution)/shard_map/convert_element_type | solution.py:80
  55.4 3.5 %collective-permute-start = (bf16[2,16384]{1,0:T(2,128)(2,1)S(1)}, bf16[2,16384]{1,0:T(2,128)(2,1)S(1)}, u32[]{:S(2)}, u32[]{:S(2)}) collective-permute-start(bf16[2,16384]{1,0:T(2,128)(2,1)S(1)} %convolution_convert_fusion.1), channel_id=1, source_target_pairs={{0,4},{4,8},{8,12},{1,5},{5,9},{9,13},{2,6},{6,10},{10,14},{3,7},{... | collective-permute-start | bytes 196616 | tf_op jit(solution)/shard_map/ppermute | solution.py:15
  58.9 0.3 convolution_convert_fusion
  59.2 1.3 collective-permute-start.1
  60.5 0.3 collective-permute-done
  60.8 4.6 %collective-permute-done.1 = bf16[2,16384]{1,0:T(2,128)(2,1)S(1)} collective-permute-done((bf16[2,16384]{1,0:T(2,128)(2,1)S(1)}, bf16[2,16384]{1,0:T(2,128)(2,1)S(1)}, u32[]{:S(2)}, u32[]{:S(2)}) %collective-permute-start.1) | collective-permute-done | bytes 65568 | tf_op jit(solution)/shard_map/ppermute | solution.py:15
  65.6 0.8 copy.78
  66.5 3.6 %all-to-all-start = ((bf16[8,32,512]{2,1,0:T(8,128)(2,1)}), bf16[8,32,512]{2,1,0:T(8,128)(2,1)S(1)}, u32[]{:S(2)}, u32[]{:S(2)}) async-start(bf16[8,32,512]{2,1,0:T(8,128)(2,1)} %copy.78), calls=%async_computation | async-start | bytes 524288 | tf_op jit(solution)/shard_map/all_to_all | solution.py:134
  70.2 24.2 %all-gather.2.cloned.1.call-done = bf16[32,32,512]{2,1,0:T(8,128)(2,1)} async-done(((bf16[8,32,512]{2,1,0:T(8,128)(2,1)}), bf16[32,32,512]{2,1,0:T(8,128)(2,1)}) %all-gather.2.cloned.1.call-update) | async-done | bytes 1048592 | tf_op jit(solution)/shard_map/all_gather | solution.py:118
  94.4 4.6 %copy.82 = bf16[32,32,512]{1,2,0:T(8,128)(2,1)} copy(bf16[32,32,512]{2,1,0:T(8,128)(2,1)} %all-gather.2.cloned.1.call-done) | data formatting | bytes 2097152 | tf_op jit(solution)/shard_map/all_gather | solution.py:118
  99.0 2.4 %fusion.92 = (bf16[32,32,1,8,8]{1,4,3,2,0:T(8,128)(2,1)}, bf16[32,32,1,8,8]{1,4,3,2,0:T(8,128)(2,1)}) fusion(bf16[32,32,8,8,8]{1,4,3,2,0:T(8,128)(2,1)} %bitcast.263), kind=kLoop, calls=%fused_computation.144 | loop fusion | bytes 524288 | tf_op jit(solution)/shard_map/slice | solution.py:32
  101.4 2.3 %fusion.91 = (bf16[32,32,8,1,8]{1,4,3,2,0:T(8,128)(2,1)}, bf16[32,32,8,1,8]{1,4,3,2,0:T(8,128)(2,1)}) fusion(bf16[32,32,8,8,8]{1,4,3,2,0:T(8,128)(2,1)} %bitcast.264), kind=kLoop, calls=%fused_computation.143 | loop fusion | bytes 524288 | tf_op jit(solution)/shard_map/slice | solution.py:34
  103.7 2.2 %fusion.90 = (bf16[32,32,8,8,1]{1,4,3,2,0:T(2,128)(2,1)S(1)}, bf16[32,32,8,8,1]{1,4,3,2,0:T(2,128)(2,1)S(1)}) fusion(bf16[32,32,8,8,8]{1,4,3,2,0:T(8,128)(2,1)S(1)} %bitcast.265), kind=kLoop, calls=%fused_computation.142 | loop fusion | bytes 524288 | tf_op jit(solution)/shard_map/slice | solution.py:36
  105.9 2.1 %copy.83 = bf16[32,32,1,8,8]{0,4,3,1,2:T(8,128)(2,1)S(1)} copy(bf16[32,32,1,8,8]{1,4,3,2,0:T(8,128)(2,1)} %get-tuple-element.84) | data formatting | bytes 262144 | tf_op jit(solution)/shard_map/slice | solution.py:33
  108.2 0.7 constant_dynamic-update-slice_fusion.5
  108.8 2.1 %copy.84 = bf16[32,32,1,8,8]{0,4,3,1,2:T(8,128)(2,1)S(1)} copy(bf16[32,32,1,8,8]{1,4,3,2,0:T(8,128)(2,1)} %get-tuple-element.83) | data formatting | bytes 262144 | tf_op jit(solution)/shard_map/slice | solution.py:32
  111.1 2.1 %copy.85 = bf16[32,32,8,1,8]{0,4,2,1,3:T(8,128)(2,1)S(1)} copy(bf16[32,32,8,1,8]{1,4,3,2,0:T(8,128)(2,1)} %get-tuple-element.82) | data formatting | bytes 262144 | tf_op jit(solution)/shard_map/slice | solution.py:35
  113.2 0.8 copy.91
  114.1 2.1 %copy.86 = bf16[32,32,8,1,8]{0,4,2,1,3:T(8,128)(2,1)S(1)} copy(bf16[32,32,8,1,8]{1,4,3,2,0:T(8,128)(2,1)} %get-tuple-element.81) | data formatting | bytes 262144 | tf_op jit(solution)/shard_map/slice | solution.py:34
  116.2 0.8 copy.92
  117.1 1.1 copy.87
  118.4 1.1 copy.88
  119.7 0.7 constant_dynamic-update-slice_fusion.4
  120.3 1.6 constant_dynamic-update-slice_fusion.3
  121.9 1.6 constant_dynamic-update-slice_fusion.2
  123.5 0.7 constant_dynamic-update-slice_fusion.1
  124.1 0.7 constant_dynamic-update-slice_fusion
  124.8 1.4 convolution_convert_fusion.2
  126.2 0.4 reshape.411
  126.6 0.3 copy.107
  126.9 1.0 reshape.412
  127.9 3.6 %all-to-all-start.1 = ((bf16[8,32,384]{2,1,0:T(8,128)(2,1)}), bf16[8,32,384]{2,1,0:T(8,128)(2,1)S(1)}, u32[]{:S(2)}, u32[]{:S(2)}) async-start(bf16[8,32,384]{2,1,0:T(8,128)(2,1)} %reshape.412), calls=%async_computation.1 | async-start | bytes 393216 | tf_op jit(solution)/shard_map/all_to_all | solution.py:135
  131.5 0.7 copy.79
  132.2 0.5 reshape.409
  132.9 3.6 %all-to-all-done.1 = bf16[8,32,384]{2,1,0:T(8,128)(2,1)S(1)} async-done(((bf16[8,32,384]{2,1,0:T(8,128)(2,1)}), bf16[8,32,384]{2,1,0:T(8,128)(2,1)S(1)}, u32[]{:S(2)}, u32[]{:S(2)}) %all-to-all-start.1) | async-done | bytes 196640 | tf_op jit(solution)/shard_map/all_to_all | solution.py:135
  136.5 0.5 copy.96
  137.1 0.4 reshape.413
  138.3 1.4 scatter.26
  139.7 1.4 scatter.29
  141.1 0.4 fusion.94
  141.5 1.0 fusion.93
  148.4 0.3 multiply_convert_fusion
  148.7 0.9 copy.101
  (60 shorter events, 8.0 us)
Async XLA Ops:
  6.5 9.0 %copy-start = (bf16[8,256,128]{2,1,0:T(8,128)(2,1)S(1)}, bf16[8,256,128]{2,1,0:T(8,128)(2,1)}, u32[]{:S(2)}) copy-start(bf16[8,256,128]{2,1,0:T(8,128)(2,1)} %param.19) | copy-start | bytes 1572868
  6.5 87.9 %all-gather.2.cloned.1.call-start = ((), (), s32[]{:S(2)}) async-start(), calls=%async_computation.2 | async-start | bytes 1310720 | tf_op jit(solution)/shard_map/all_gather | solution.py:118
  36.5 18.7 %copy-start.4 = (s32[16]{0:T(128)S(1)}, s32[16]{0:T(128)}, u32[]{:S(2)}) copy-start(s32[16]{0:T(128)} %param.22) | copy-start | bytes 196
  36.5 30.0 %copy-start.3 = (s32[8,6]{1,0:T(8,128)S(1)}, s32[8,6]{1,0:T(8,128)}, u32[]{:S(2)}) copy-start(s32[8,6]{1,0:T(8,128)} %param.23) | copy-start | bytes 580
  55.4 5.4 %collective-permute-start = (bf16[2,16384]{1,0:T(2,128)(2,1)S(1)}, bf16[2,16384]{1,0:T(2,128)(2,1)S(1)}, u32[]{:S(2)}, u32[]{:S(2)}) collective-permute-start(bf16[2,16384]{1,0:T(2,128)(2,1)S(1)} %convolution_convert_fusion.1), channel_id=1, source_target_pairs={{0,4},{4,8},{8,12},{1,5},{5,9},{9,13},{2,6},{6,10},{10,14},{3,7},{... | collective-permute-start | bytes 196616 | tf_op jit(solution)/shard_map/ppermute | solution.py:15
  59.2 6.2 %collective-permute-start.1 = (bf16[2,16384]{1,0:T(2,128)(2,1)S(1)}, bf16[2,16384]{1,0:T(2,128)(2,1)S(1)}, u32[]{:S(2)}, u32[]{:S(2)}) collective-permute-start(bf16[2,16384]{1,0:T(2,128)(2,1)S(1)} %convolution_convert_fusion), channel_id=1, source_target_pairs={{4,0},{8,4},{12,8},{5,1},{9,5},{13,9},{6,2},{10,6},{14,10},{7,3},{... | collective-permute-start | bytes 196616 | tf_op jit(solution)/shard_map/ppermute | solution.py:15
  66.5 61.3 %all-to-all-start = ((bf16[8,32,512]{2,1,0:T(8,128)(2,1)}), bf16[8,32,512]{2,1,0:T(8,128)(2,1)S(1)}, u32[]{:S(2)}, u32[]{:S(2)}) async-start(bf16[8,32,512]{2,1,0:T(8,128)(2,1)} %copy.78), calls=%async_computation | async-start | bytes 524288 | tf_op jit(solution)/shard_map/all_to_all | solution.py:134
  99.0 4.7 %copy-start.1 = (bf16[32,32,512]{1,2,0:T(8,128)(2,1)S(1)}, bf16[32,32,512]{1,2,0:T(8,128)(2,1)}, u32[]{:S(2)}) copy-start(bf16[32,32,512]{1,2,0:T(8,128)(2,1)} %copy.82) | copy-start | bytes 3145732
  127.9 8.7 %all-to-all-start.1 = ((bf16[8,32,384]{2,1,0:T(8,128)(2,1)}), bf16[8,32,384]{2,1,0:T(8,128)(2,1)S(1)}, u32[]{:S(2)}, u32[]{:S(2)}) async-start(bf16[8,32,384]{2,1,0:T(8,128)(2,1)} %reshape.412), calls=%async_computation.1 | async-start | bytes 393216 | tf_op jit(solution)/shard_map/all_to_all | solution.py:135
  141.5 1.2 copy-start.2
  147.1 1.3 copy-start.5
Sparse Core Ops, SparseCore 0:
  66.6 27.7 all-gather.1
where the time goes:
time: 157 us; the launch traced here: 156 us
  local copies, waits for them, and re-layouts  80.2 us (51%)
  waiting for transfers between devices  32.7 us (21%)
  between operations  13.9 us (9%)
  starting transfers between devices  12 us (8%)
  blocking collectives  8.95 us (6%)
  matrix products  8.52 us (5%)
    convert_element_type x3, local copies, waits for them, and re-layouts, per_device(): candidates = spread_children(spread).astype(jnp.bfloat16)  37.3 us
    all_gather x1, waiting for transfers between devices, per_device(): layers = face_slabs(lax.all_gather(blocks, 'morton', axis=0, tiled=True))  24.2 us
    all_gather x1, blocking collectives, per_device(): lax.all_gather(parents, 'chan', axis=1, tiled=True)  8.95 us
    dot_general x27, matrix products, convolve(): jnp.einsum('cd,bcv->bdv', weight_tap, tap_view, preferred_element_type=jn...  5.8 us
    unnamed x18, local copies, waits for them, and re-layouts  5.34 us
    ppermute x2, waiting for transfers between devices, passed_along(): return lax.ppermute(block, axis, route)  4.86 us
    ppermute x2, starting transfers between devices, passed_along(): return lax.ppermute(block, axis, route)  4.78 us
    all_gather x1, local copies, waits for them, and re-layouts, per_device(): layers = face_slabs(lax.all_gather(blocks, 'morton', axis=0, tiled=True))  4.58 us
  transfers between devices with their start and end apart: 5, of which 4 were waited for; matrix products, arithmetic and copies ran while one was open for 22% of the time, Pallas kernels for 0%

commit v1 on v0

v1 whole, which is shorter than its diff:
```python
import functools

import jax
import jax.numpy as jnp
import numpy as np
from jax import lax
from jax.experimental import pallas as pl
from jax.experimental.pallas import tpu as pltpu
from jax.sharding import PartitionSpec as P

MOVE_CAP = 2
FACE_CAP = 4
PIECE = 64
LAYER = 16
MESH = pl.DeviceIdType.MESH


def layer_voxels():
    p, q = np.divmod(np.arange(LAYER), 4)
    return np.stack(
        [48 + 4 * p + q, 4 * p + q, 16 * p + 12 + q, 16 * p + q, 16 * p + 4 * q + 3, 16 * p + 4 * q]
    ).astype(np.int32)


def piece_lanes():
    v = np.arange(PIECE)
    base = 64 * (v // 16) + 8 * (v // 4 % 4) + v % 4
    k = np.arange(8)
    return base.astype(np.int32), (256 * (k % 2) + 32 * (k // 2 % 2) + 4 * (k // 4)).astype(np.int32)


def tables(child_dest, face_nbr, ranges, chans):
    block_count = face_nbr.shape[0]
    own_blocks = block_count // chans
    me = lax.axis_index("morton")
    mine = lax.axis_index("chan")
    base, octant = piece_lanes()
    cand = np.arange(child_dest.shape[0])
    cand_lane = jnp.asarray(512 * (cand // 8) + octant[cand % 8], jnp.int32)

    slots = np.concatenate(
        [
            np.arange(block_count),
            block_count + np.arange(MOVE_CAP),
            np.arange(MOVE_CAP) - MOVE_CAP,
        ]
    ).astype(np.int32)
    wanted = me * block_count + jnp.asarray(slots)
    match = (child_dest[None, :] == wanted[:, None]) & (child_dest >= 0)[None, :]
    found = jnp.sum(jnp.where(match, cand_lane[None, :] + 1, 0), axis=1) - 1
    pick = jnp.where(found[:, None] >= 0, found[:, None] + jnp.asarray(base)[None, :], -1)
    pick = pick.reshape(1, -1)

    entries = face_nbr.reshape(chans, own_blocks * 6)
    count = own_blocks * 6
    face = np.arange(count) % 6
    layer = layer_voxels()
    home = jnp.where(entries >= 0, entries // block_count, -1)
    earlier = np.tril(np.ones((count, count), bool), -1)
    rank = jnp.sum(
        ((home[:, :, None] == home[:, None, :]) & jnp.asarray(earlier)[None]).astype(jnp.int32), axis=2
    )
    offset = jnp.where(home >= 0, lax.rem(home - me + ranges, ranges), -1)
    start = lax.rem(entries, block_count) * PIECE
    far = jnp.arange(1, ranges, dtype=jnp.int32)
    slot_ids = jnp.arange(FACE_CAP, dtype=jnp.int32)
    asks = (offset[None, :, None, :] == far[:, None, None, None]) & (
        rank[None, :, None, :] == slot_ids[None, None, :, None]
    )
    value = start[:, None, :] + jnp.asarray(layer[face].T)[None] + 1
    request = (
        jnp.sum(jnp.where(asks[:, :, :, None, :], value[None, :, None, :, :], 0), axis=-1) - 1
    ).reshape(ranges - 1, 1, chans * FACE_CAP * LAYER)

    def own(a):
        return lax.dynamic_slice_in_dim(a, mine, 1, 0).reshape(own_blocks, 6)

    o_off, o_start, o_rank = own(offset), own(start), own(rank)
    w = np.arange(8)
    inner = (PIECE * (mine * own_blocks + jnp.arange(own_blocks, dtype=jnp.int32)))[:, None] + jnp.asarray(
        (np.arange(16)[:, None] * 4 + w[None, :] // 2).reshape(1, 128).astype(np.int32)
    )
    near = o_off == 0
    spot = jnp.where(
        near, o_start, block_count * PIECE + (o_off - 1) * FACE_CAP * LAYER + o_rank * LAYER
    )
    side16 = (np.arange(4)[:, None] * 4 + w[None, :] // 2).reshape(32).astype(np.int32)
    side_vox = layer[:4][:, side16]
    sides = spot[:, :4, None] + jnp.where(near[:, :4, None], jnp.asarray(side_vox)[None], jnp.asarray(side16))
    sides = jnp.where(o_off[:, :4, None] >= 0, sides, -1).reshape(own_blocks, 128)
    ends = spot[:, 4:, None] + jnp.where(
        near[:, 4:, None], jnp.asarray(layer[4:])[None], jnp.arange(LAYER, dtype=jnp.int32)
    )
    ends = jnp.where(o_off[:, 4:, None] >= 0, ends, -1)
    caps = jnp.where(
        jnp.asarray(w == 0),
        ends[:, 0, :, None],
        jnp.where(jnp.asarray(w == 7), ends[:, 1, :, None], -1),
    ).reshape(own_blocks, 128)
    rows = jnp.concatenate([inner, sides, caps], axis=1).reshape(1, own_blocks * 384)
    return pick, request, rows


def one_hot(depth, target, first=0):
    shape = (depth, target.shape[1])
    lanes = lax.broadcasted_iota(jnp.int32, shape, 0) + first
    return jnp.where(lanes == target, 1.0, 0.0).astype(jnp.bfloat16)


def each(count, body):
    if count <= 4:
        for i in range(count):
            body(i)
    else:
        lax.fori_loop(0, count, lambda i, c: (body(i), c)[1], 0)


def kernel(
    ranges,
    chans,
    parents_ref,
    pick_ref,
    request_ref,
    rows_ref,
    bias_ref,
    up_hbm,
    conv_hbm,
    out_ref,
    up_ref,
    conv_ref,
    moves,
    moved,
    asked,
    held,
    faces_out,
    faces_in,
    far_ref,
    cube,
    cols,
    load_sem,
    ask_send,
    ask_recv,
    move_send,
    move_recv,
    held_send,
    held_recv,
    face_send,
    face_recv,
):
    me = lax.axis_index("morton")
    mine = lax.axis_index("chan")
    total = ranges * chans
    own_blocks = out_ref.shape[0]
    parent_count, depth = parents_ref.shape[0], parents_ref.shape[1]
    half = depth // 2
    width = held.shape[2]

    up_load = pltpu.make_async_copy(up_hbm, up_ref, load_sem.at[0])
    conv_load = pltpu.make_async_copy(conv_hbm, conv_ref, load_sem.at[1])
    up_load.start()
    conv_load.start()

    def at(range_id, chan_id):
        return {"morton": range_id, "chan": chan_id}

    barrier = pltpu.get_barrier_semaphore()
    here = me * chans + mine

    def greet(i):
        other = lax.rem(here + i + 1, total)
        pl.semaphore_signal(
            barrier, inc=1, device_id=at(other // chans, lax.rem(other, chans)), device_id_type=MESH
        )

    each(total - 1, greet)

    gathered = jnp.zeros((depth, pick_ref.shape[1]), jnp.float32)
    for p in range(parent_count):
        gathered = gathered + jnp.dot(
            parents_ref[p],
            one_hot(512, pick_ref[...], 512 * p),
            preferred_element_type=jnp.float32,
        )
    move_width = MOVE_CAP * PIECE
    moves[0] = gathered[:, width : width + move_width].astype(jnp.bfloat16)
    moves[1] = gathered[:, width + move_width :].astype(jnp.bfloat16)
    faces_in[ranges - 1] = jnp.zeros(faces_in.shape[1:], jnp.bfloat16)

    pl.semaphore_wait(barrier, total - 1)

    def move_copy(side):
        other = lax.rem(me + (1 if side == 0 else ranges - 1), ranges)
        return pltpu.make_async_remote_copy(
            src_ref=moves.at[side],
            dst_ref=moved.at[side],
            send_sem=move_send.at[side],
            recv_sem=move_recv.at[side],
            device_id=at(other, mine),
            device_id_type=MESH,
        )

    def ask_copy(m):
        return pltpu.make_async_remote_copy(
            src_ref=request_ref.at[m],
            dst_ref=asked.at[ranges - 2 - m],
            send_sem=ask_send.at[m],
            recv_sem=ask_recv.at[ranges - 2 - m],
            device_id=at(lax.rem(me + m + 1, ranges), mine),
            device_id_type=MESH,
        )

    move_copy(0).start()
    move_copy(1).start()
    each(ranges - 1, lambda m: ask_copy(m).start())

    for side in range(2):
        move_copy(side).wait()
    up_part = jnp.concatenate(
        [moved[0].astype(jnp.float32), jnp.zeros((depth, width - move_width), jnp.float32)], axis=1
    )
    down_part = jnp.concatenate(
        [jnp.zeros((depth, width - move_width), jnp.float32), moved[1].astype(jnp.float32)], axis=1
    )
    blocks = (gathered[:, :width] + up_part + down_part).astype(jnp.bfloat16)
    held[mine] = blocks

    def held_copy(i):
        peer = lax.rem(mine + i + 1, chans)
        return pltpu.make_async_remote_copy(
            src_ref=held.at[mine],
            dst_ref=held.at[mine],
            send_sem=held_send.at[i],
            recv_sem=held_recv.at[i],
            device_id=at(me, peer),
            device_id_type=MESH,
        )

    each(chans - 1, lambda i: held_copy(i).start())

    def face_copy(m, j):
        return pltpu.make_async_remote_copy(
            src_ref=faces_out.at[m, j],
            dst_ref=faces_in.at[ranges - 2 - m, mine],
            send_sem=face_send.at[m, j],
            recv_sem=face_recv.at[ranges - 2 - m, mine],
            device_id=at(lax.rem(me + m + 1, ranges), j),
            device_id_type=MESH,
        )

    def answer(m):
        pltpu.make_async_remote_copy(
            src_ref=request_ref.at[m],
            dst_ref=asked.at[m],
            send_sem=ask_send.at[m],
            recv_sem=ask_recv.at[m],
            device_id=at(lax.rem(me + m + 1, ranges), mine),
            device_id_type=MESH,
        ).wait()
        found = jnp.dot(
            held[mine], one_hot(width, asked[m]), preferred_element_type=jnp.float32
        )
        for j in range(chans):
            part = found[:, PIECE * j : PIECE * (j + 1)]
            faces_out[m, j] = jnp.concatenate([part[:half], part[half:]], axis=1).astype(jnp.bfloat16)
            face_copy(m, j).start()

    each(ranges - 1, answer)

    up_load.wait()
    each(chans - 1, lambda i: held_copy(i).wait_send())

    def held_wait(i):
        source = lax.rem(mine + chans - i - 1, chans)
        pltpu.make_async_remote_copy(
            src_ref=held.at[source],
            dst_ref=held.at[source],
            send_sem=held_send.at[i],
            recv_sem=held_recv.at[i],
            device_id=at(me, source),
            device_id_type=MESH,
        ).wait_recv()

    each(chans - 1, held_wait)
    near = jnp.dot(
        held[...].reshape(chans * depth, width),
        one_hot(width, rows_ref[...]),
        preferred_element_type=jnp.float32,
    )

    def face_wait(m):
        for j in range(chans):
            face_copy(m, j).wait_send()
            pltpu.make_async_remote_copy(
                src_ref=faces_out.at[m, j],
                dst_ref=faces_in.at[m, j],
                send_sem=face_send.at[m, j],
                recv_sem=face_recv.at[m, j],
                device_id=at(lax.rem(me + m + 1, ranges), j),
                device_id_type=MESH,
            ).wait_recv()

    each(ranges - 1, face_wait)

    def unpack(m):
        both = faces_in[m].astype(jnp.float32)
        part = jnp.concatenate([both[:, :, :PIECE], both[:, :, PIECE:]], axis=1)
        return part.reshape(chans * depth, PIECE)

    def widen(i):
        lanes = pl.ds(i * 2 * PIECE if isinstance(i, int) else pl.multiple_of(i * 2 * PIECE, 2 * PIECE), 2 * PIECE)
        far_ref[:, lanes] = jnp.concatenate([unpack(2 * i), unpack(2 * i + 1)], axis=1).astype(jnp.bfloat16)

    each(ranges // 2, widen)
    chosen = near + jnp.dot(
        far_ref[...],
        one_hot(far_ref.shape[1], rows_ref[...], width),
        preferred_element_type=jnp.float32,
    )
    chosen = chosen.T.astype(jnp.bfloat16)

    count = own_blocks * 384
    row = lax.broadcasted_iota(jnp.int32, (count, 128), 0)
    odd = lax.rem(row, 2) == 1
    cap = lax.rem(row // 128, 3) == 2
    high = jnp.logical_xor(odd, cap)
    z_at = lax.rem(lax.broadcasted_iota(jnp.int32, (128, 128), 0), 8)
    lifted = {}
    for ox in range(2):
        for oy in range(2):
            low_z = jnp.dot(chosen, up_ref[4 * ox + 2 * oy], preferred_element_type=jnp.float32)
            high_z = jnp.dot(chosen, up_ref[4 * ox + 2 * oy + 1], preferred_element_type=jnp.float32)
            lifted[ox, oy] = jnp.where(high, high_z, low_z)

    nothing = jnp.zeros((8, 128), jnp.float32)

    def shifts(middle, end):
        below = jnp.where(z_at == 0, end, pltpu.roll(middle, 1, 0))
        above = jnp.where(z_at == 7, end, pltpu.roll(middle, 127, 0))
        return below, middle, above

    conv_load.wait()
    for b in range(own_blocks):
        first = 384 * b
        for ox in range(2):
            for oy in range(2):
                plane = lifted[ox, oy]
                inner = shifts(plane[first : first + 128], plane[first + 256 : first + 384])
                sides = shifts(plane[first + 128 : first + 256], 0.0)
                for dz in range(3):
                    for p in range(4):
                        for q in range(4):
                            at_row = 8 * (4 * p + q)
                            cube[dz, 1 + 2 * p + ox, 1 + 2 * q + oy] = inner[dz][at_row : at_row + 8]
                    for t in range(4):
                        face_x, face_y = 1 - ox, 3 - oy
                        low = 32 * face_x + 8 * t
                        cube[dz, 9 * face_x, 1 + 2 * t + oy] = sides[dz][low : low + 8]
                        low = 32 * face_y + 8 * t
                        cube[dz, 1 + 2 * t + ox, 9 * (face_y - 2)] = sides[dz][low : low + 8]
        for dz in range(3):
            for x in (0, 9):
                for y in (0, 9):
                    cube[dz, x, y] = nothing
        for x in range(10):
            for dy in range(3):
                for dz in range(3):
                    lane = 128 * (3 * dy + dz)
                    cols[x, :, lane : lane + 128] = (
                        cube[dz, x, dy : dy + 8].reshape(64, 128).astype(jnp.bfloat16)
                    )
        total_sum = jnp.zeros((512, 128), jnp.float32) + bias_ref[...]
        for dx in range(3):
            total_sum = total_sum + jnp.dot(
                cols[dx : dx + 8].reshape(512, 1152),
                conv_ref[9 * dx : 9 * dx + 9].reshape(1152, 128),
                preferred_element_type=jnp.float32,
            )
        result = total_sum / (1.0 + jnp.exp(-total_sum))
        out_ref[b] = result.T.astype(jnp.bfloat16)


def per_device(parents, up_weight, conv_weight, conv_bias, child_dest, face_nbr):
    ranges, chans = lax.axis_size("morton"), lax.axis_size("chan")
    block_count = face_nbr.shape[0]
    own_blocks = block_count // chans
    depth = parents.shape[1]
    width = block_count * PIECE
    pick, request, rows = tables(child_dest, face_nbr, ranges, chans)
    vmem = pl.BlockSpec(memory_space=pltpu.VMEM)
    anywhere = pl.BlockSpec(memory_space=pl.ANY)
    bf16 = jnp.bfloat16
    dma = pltpu.SemaphoreType.DMA
    return pl.pallas_call(
        functools.partial(kernel, ranges, chans),
        out_shape=jax.ShapeDtypeStruct((own_blocks, 128, 512), bf16),
        in_specs=[vmem] * 5 + [anywhere] * 2,
        out_specs=vmem,
        scratch_shapes=[
            pltpu.VMEM(up_weight.shape, bf16),
            pltpu.VMEM(conv_weight.shape, bf16),
            pltpu.VMEM((2, depth, MOVE_CAP * PIECE), bf16),
            pltpu.VMEM((2, depth, MOVE_CAP * PIECE), bf16),
            pltpu.VMEM(request.shape, jnp.int32),
            pltpu.VMEM((chans, depth, width), bf16),
            pltpu.VMEM((ranges - 1, chans, depth // 2, 2 * PIECE), bf16),
            pltpu.VMEM((ranges, chans, depth // 2, 2 * PIECE), bf16),
            pltpu.VMEM((chans * depth, ranges * PIECE), bf16),
            pltpu.VMEM((3, 10, 10, 8, 128), jnp.float32),
            pltpu.VMEM((10, 64, 1152), bf16),
            dma((2,)),
            dma((ranges - 1,)),
            dma((ranges - 1,)),
            dma((2,)),
            dma((2,)),
            dma((chans - 1,)),
            dma((chans - 1,)),
            dma((ranges - 1, chans)),
            dma((ranges - 1, chans)),
        ],
        compiler_params=pltpu.CompilerParams(
            collective_id=0, has_side_effects=True, vmem_limit_bytes=40 * 1024 * 1024
        ),
        name="sparse_level",
    )(parents, pick, request, rows, conv_bias.reshape(1, -1), up_weight, conv_weight)


def solution(mesh):
    placed = (
        P(("groups", "morton"), "chan", None),
        P(),
        P(),
        P(),
        P(("groups", "morton")),
        P(("groups", "morton"), None),
    )
    return jax.shard_map(
        per_device,
        mesh=mesh,
        in_specs=placed,
        out_specs=P(("groups", "morton", "chan"), None, None),
        check_vma=False,
    )
```

time: 157 us -> 29.9 us (0.19)
  local copies, waits for them, and re-layouts: 80.2 us -> 6.91 us
  waiting for transfers between devices: 32.7 us -> 0 us
  Pallas kernels: 0 us -> 18.1 us
  between operations: 13.9 us -> 0.2 us
  starting transfers between devices: 12 us -> 0 us
  blocking collectives: 8.95 us -> 0 us
  matrix products: 8.52 us -> 0 us
  other arithmetic: 0.03 us -> 4.34 us
    convert_element_type x4 -> x0, local copies, waits for them, and re-layouts: 38.2 us -> none  [the longest x3 37.3 us: per_device(): candidates = spread_children(spread).astype(jnp.bfloat16)]
    all_gather x1 -> x0, waiting for transfers between devices: 24.2 us -> none  [per_device(): layers = face_slabs(lax.all_gather(blocks, 'morton', axis=0, tiled=True))]
    slice x11 -> x4, local copies, waits for them, and re-layouts: 19 us -> 0.36 us  [the longest x2 0.19 us: tables(): near[:, 4:, None]]
    pallas_call x0 -> x1, Pallas kernels: none -> 18.1 us  [per_device(): pl.pallas_call(functools.partial(kernel, ranges, chans), out_shape=jax.Sh...]
    all_gather x1 -> x0, blocking collectives: 8.95 us -> none  [per_device(): lax.all_gather(parents, 'chan', axis=1, tiled=True)]
    dot_general x32 -> x0, matrix products: 8.52 us -> none  [the longest x27 5.8 us: convolve(): jnp.einsum('cd,bcv->bdv', weight_tap, tap_view, preferred_element_type=jn...]
    all_to_all x2 -> x0, starting transfers between devices: 7.25 us -> none  [the longest x1 3.63 us: per_device(): lax.all_to_all(blocks, 'chan', split_axis=0, concat_axis=1, tiled=True)]
    ppermute x2 -> x0, waiting for transfers between devices: 4.86 us -> none  [passed_along(): return lax.ppermute(block, axis, route)]
  transfers between devices with their start and end apart: 5 -> 0, of which waited for: 4 -> 0; matrix products, arithmetic and copies ran while one was open for 22% -> 0% of each run, Pallas kernels for 0% -> 0%
where the time goes in v1:
time: 29.9 us; the launch traced here: 29.6 us
  Pallas kernels  18.1 us (61%)
  local copies, waits for them, and re-layouts  6.91 us (23%)
  other arithmetic  4.34 us (15%)
    pallas_call x1, Pallas kernels, per_device(): pl.pallas_call(functools.partial(kernel, ranges, chans), out_shape=jax.Sh...  18.1 us
    unnamed x28, local copies, waits for them, and re-layouts  3.95 us
    reduce_sum x1, other arithmetic, tables(): found = jnp.sum(jnp.where(match, cand_lane[None, :] + 1, 0), axis=1) - 1  0.84 us
    add x1, other arithmetic, tables(): value = start[:, None, :] + jnp.asarray(layer[face].T)[None] + 1  0.77 us
    reshape x1, local copies, waits for them, and re-layouts, tables(): entries = face_nbr.reshape(chans, own_blocks * 6)  0.77 us
    select_n x1, other arithmetic, tables(): jnp.where(o_off[:, :4, None] >= 0, sides, -1).reshape(own_blocks, 128)  0.67 us
    ge x1, other arithmetic, tables(): child_dest >= 0  0.66 us

profile of v1, /device:TPU:0, one launch (start us, length us, event | category | flops | bytes accessed | tf_op | source)
XLA Modules:
  0.0 29.6 jit_solution(7663112599134354456)
XLA Ops:
  0.0 0.0 copy-start.7
  0.1 0.6 %copy-done.12 = s32[12]{0:T(128)S(1)} copy-done((s32[12]{0:T(128)S(1)}, s32[12]{0:T(128)}, u32[]{:S(2)}) %copy-start.12) | copy-done | bytes 72
  0.7 0.0 copy-done.11
  0.7 0.1 broadcast_add_fusion.1
  0.7 0.7 %broadcast_compare_fusion.3 = pred[16]{0:T(512)(128)(4,1)S(1)} fusion(s32[16]{0:T(128)} %param.21), kind=kLoop, calls=%fused_computation.41 | loop fusion | flops 16 | bytes 80 | tf_op jit(solution)/shard_map/ge | solution.py:49
  1.4 0.8 %select_reduce_fusion.1 = s32[12]{0:T(128)S(1)} fusion(s32[16]{0:T(128)S(1)} %copy-done.10, s32[16]{0:T(128)} %param.21, s32[12]{0:T(128)S(1)} %broadcast_add_fusion.3, pred[16]{0:T(512)(128)(4,1)S(1)} %broadcast_compare_fusion.3), kind=kLoop, calls=%fused_computation.8 | loop fusion | flops 756 | bytes 240 | tf_op jit(solution)/shard_map/reduce_sum | solution.py:50
  2.3 0.1 broadcast_in_dim.204
  2.4 0.1 broadcast_in_dim.208
  2.5 0.1 broadcast_in_dim.219
  2.6 0.8 %reshape.250 = s32[4,12]{1,0:T(4,128)S(1)} reshape(s32[8,6]{1,0:T(8,128)} %param.22) | data formatting | bytes 384 | tf_op jit(solution)/shard_map/reshape | solution.py:54
  3.4 0.1 broadcast_compare_fusion
  3.5 0.1 reshape.251
  3.6 0.1 slice.29
  3.7 0.1 copy.33
  3.8 0.1 slice_compare_fusion
  3.8 0.1 copy.31
  4.0 0.1 broadcast_in_dim.197
  4.0 0.1 broadcast_in_dim.198
  4.1 0.1 broadcast_in_dim.199
  4.2 0.1 broadcast_in_dim.200
  4.3 0.1 reshape.252
  4.4 0.1 add_select_fusion
  4.4 0.1 select_n.101.pick_ref
  4.5 0.1 copy.29
  4.6 0.4 %convert_reduce_fusion = s32[4,12]{0,1:T(8,128)S(1)} fusion(s32[4,12]{1,0:T(4,128)S(1)} %get-tuple-element.6, s32[4,12]{0,1:T(8,128)S(1)} %copy.29, pred[12,12]{1,0:T(8,128)(4,1)S(1)} %copy-done.4), kind=kLoop, calls=%fused_computation.4 | loop fusion | flops 2256 | bytes 720 | tf_op jit(solution)/shard_map/reduce_sum | solution.py:60
  5.0 0.2 multiply_reduce_fusion
  5.2 0.1 copy.30
  5.3 0.1 mul.43
  5.4 0.1 slice.28
  5.4 0.1 copy.32
  5.5 0.1 add_select_fusion.2
  5.6 0.1 add.180
  5.7 0.1 add.181
  5.8 0.7 %add_select_fusion.3 = s32[2,128]{1,0:T(2,128)S(1)} fusion(pred[2,128]{1,0:T(4,128)(4,1)S(1)} %broadcast_in_dim.198, s32[2,128]{1,0:T(2,128)S(1)} %add.181, pred[2,128]{1,0:T(4,128)(4,1)S(1)} %broadcast_in_dim.200, s32[128]{0:T(128)S(1)} %broadcast_in_dim.204, s32[128]{0:T(128)} %constant.94), kind=kLoop, calls=%fused_computation.28 | loop fusion | flops 768 | bytes 3584 | tf_op jit(solution)/shard_map/jit(_where)/select_n | solution.py:90
  6.4 0.1 iota_compare_fusion
  6.5 0.1 broadcast_and_fusion
  6.6 0.1 broadcast_in_dim.222
  6.7 0.1 broadcast_in_dim.223
  6.8 0.1 broadcast_in_dim.216
  6.8 0.1 broadcast_in_dim.217
  7.0 0.8 %add_add_fusion = s32[4,16,12]{1,2,0:T(8,128)S(1)} fusion(s32[16,12]{0,1:T(8,128)} %constant.84.clone, s32[4,12]{1,0:T(4,128)S(1)} %get-tuple-element.9), kind=kLoop, calls=%fused_computation.2 | loop fusion | flops 1536 | bytes 4032 | tf_op jit(solution)/shard_map/add | solution.py:70
  7.8 0.2 select_reduce_fusion
  8.0 0.1 sub.33.request_ref
  8.1 0.6 %copy-done.3 = f32[128]{0:T(128)S(1)} copy-done((f32[128]{0:T(128)S(1)}, f32[128]{0:T(128)}, u32[]{:S(2)}) %copy-start.3) | copy-done | bytes 536
  8.7 1.2 %copy-done = bf16[27,128,128]{2,1,0:T(8,128)(2,1)S(1)} copy-done((bf16[27,128,128]{2,1,0:T(8,128)(2,1)S(1)}, bf16[27,128,128]{2,1,0:T(8,128)(2,1)}, u32[]{:S(2)}) %copy-start) | copy-done | bytes 884760
  9.8 0.9 %copy-done.2 = bf16[2,64,512]{2,1,0:T(8,128)(2,1)S(1)} copy-done((bf16[2,64,512]{2,1,0:T(8,128)(2,1)S(1)}, bf16[2,64,512]{2,1,0:T(8,128)(2,1)}, u32[]{:S(2)}) %copy-start.2) | copy-done | bytes 131096
  10.7 18.1 %sparse_level.1 = bf16[2,128,512]{2,1,0:T(8,128)(2,1)S(1)} custom-call(bf16[2,64,512]{2,1,0:T(8,128)(2,1)S(1)} %copy-done.2, s32[1,768]{1,0:T(1,128)S(1)} %select_n.101.pick_ref, s32[3,1,256]{2,1,0:T(1,128)S(1)} %sub.33.request_ref, s32[1,768]{1,0:T(1,128)S(1)} %bitcast.11, f32[1,128]{1,0:T(1,128)S(1)} %bitcast.12, bf16[8,256,128]{2,1,0:T(8,128)(2,1)S(1)} %copy-done.1, ...), custom_call_target="tpu_custom_call" | custom-call | tf_op jit(solution)/shard_map/sparse_level/pallas_call | solution.py:393
  28.9 0.7 %copy.36 = bf16[2,128,512]{2,1,0:T(8,128)(2,1)} copy(bf16[2,128,512]{2,1,0:T(8,128)(2,1)S(1)} %sparse_level.1) | data formatting | bytes 524288
  (38 shorter events, 0.2 us)
Async XLA Ops:
  0.0 0.7 %copy-start.12 = (s32[12]{0:T(128)S(1)}, s32[12]{0:T(128)}, u32[]{:S(2)}) copy-start(s32[12]{0:T(128)} %constant.81.clone) | copy-start | bytes 148
  0.0 0.7 %copy-start.11 = (s32[128]{0:T(128)S(1)}, s32[128]{0:T(128)}, u32[]{:S(2)}) copy-start(s32[128]{0:T(128)} %constant.93) | copy-start | bytes 1540
  0.0 1.4 %copy-start.10 = (s32[16]{0:T(128)S(1)}, s32[16]{0:T(128)}, u32[]{:S(2)}) copy-start(s32[16]{0:T(128)} %constant.92) | copy-start | bytes 196
  0.0 2.3 %copy-start.9 = (s32[32]{0:T(128)S(1)}, s32[32]{0:T(128)}, u32[]{:S(2)}) copy-start(s32[32]{0:T(128)} %constant.87.clone) | copy-start | bytes 388
  0.0 2.4 %copy-start.8 = (pred[8]{0:T(512)(128)(4,1)S(1)}, pred[8]{0:T(512)(128)(4,1)}, u32[]{:S(2)}) copy-start(pred[8]{0:T(512)(128)(4,1)} %constant.89.clone) | copy-start | bytes 28
  0.0 2.5 %copy-start.7 = (pred[8]{0:T(512)(128)(4,1)S(1)}, pred[8]{0:T(512)(128)(4,1)}, u32[]{:S(2)}) copy-start(pred[8]{0:T(512)(128)(4,1)} %constant.90.clone) | copy-start | bytes 28
  0.0 4.3 %copy-start.6 = (s32[64]{0:T(128)S(1)}, s32[64]{0:T(128)}, u32[]{:S(2)}) copy-start(s32[64]{0:T(128)} %constant.82.clone) | copy-start | bytes 772
  0.0 4.6 %copy-start.4 = (pred[12,12]{1,0:T(8,128)(4,1)S(1)}, pred[12,12]{1,0:T(8,128)(4,1)}, u32[]{:S(2)}) copy-start(pred[12,12]{1,0:T(8,128)(4,1)} %constant.83.clone) | copy-start | bytes 436
  0.1 5.5 %copy-start.5 = (s32[2,16]{1,0:T(2,128)S(1)}, s32[2,16]{1,0:T(2,128)}, u32[]{:S(2)}) copy-start(s32[2,16]{1,0:T(2,128)} %constant.88.clone) | copy-start | bytes 388
  0.1 8.0 %copy-start.1 = (bf16[8,256,128]{2,1,0:T(8,128)(2,1)S(1)}, bf16[8,256,128]{2,1,0:T(8,128)(2,1)}, u32[]{:S(2)}) copy-start(bf16[8,256,128]{2,1,0:T(8,128)(2,1)} %up_hbm.1) | copy-start | bytes 1572868
  8.0 0.7 %copy-start.3 = (f32[128]{0:T(128)S(1)}, f32[128]{0:T(128)}, u32[]{:S(2)}) copy-start(f32[128]{0:T(128)} %param.20) | copy-start | bytes 1540
  8.7 1.2 %copy-start = (bf16[27,128,128]{2,1,0:T(8,128)(2,1)S(1)}, bf16[27,128,128]{2,1,0:T(8,128)(2,1)}, u32[]{:S(2)}) copy-start(bf16[27,128,128]{2,1,0:T(8,128)(2,1)} %conv_hbm.1) | copy-start | bytes 2654212
  9.8 0.9 %copy-start.2 = (bf16[2,64,512]{2,1,0:T(8,128)(2,1)S(1)}, bf16[2,64,512]{2,1,0:T(8,128)(2,1)}, u32[]{:S(2)}) copy-start(bf16[2,64,512]{2,1,0:T(8,128)(2,1)} %parents_ref.1) | copy-start | bytes 393220

commit v2 on v1

v2 whole, which is shorter than its diff:
```python
import functools

import jax
import jax.numpy as jnp
from jax import lax
from jax.experimental import pallas as pl
from jax.experimental.pallas import tpu as pltpu
from jax.sharding import PartitionSpec as P

MOVE_CAP = 2
FACE_CAP = 4
PIECE = 64
LAYER = 16
MESH = pl.DeviceIdType.MESH


def lane_ids(width, rows=1):
    return lax.broadcasted_iota(jnp.int32, (rows, width), 1)


def layer_voxel(face, place):
    p, q = place >> 2, place & 3
    return (
        lambda: 48 + place,
        lambda: place,
        lambda: 16 * p + 12 + q,
        lambda: 16 * p + q,
        lambda: 4 * place + 3,
        lambda: 4 * place,
    )[face]()


def pick_table(dest_ref, ranges, block_count, me):
    slots = block_count + 2 * MOVE_CAP
    lane = lane_ids(slots * PIECE)
    slot, v = lane // PIECE, lane % PIECE
    slot = jnp.where(slot < block_count + MOVE_CAP, slot, slot - slots)
    wanted = me * block_count + slot
    wanted = jnp.where(wanted < 0, -9, wanted)
    base = 64 * (v // 16) + 8 * (v // 4 % 4) + v % 4
    pick = jnp.full(lane.shape, -1, jnp.int32)
    for c in range(dest_ref.shape[0]):
        k = c % 8
        first = 512 * (c // 8) + 256 * (k % 2) + 32 * (k // 2 % 2) + 4 * (k // 4)
        pick = jnp.where(wanted == dest_ref[c], base + first, pick)
    return pick


def request_table(nbr_ref, ranges, chans, me):
    block_count = nbr_ref.shape[0]
    own_blocks = block_count // chans
    shape = (ranges - 1, chans * FACE_CAP * LAYER)
    lane = lane_ids(shape[1], shape[0])
    device, slot, place = lane // (FACE_CAP * LAYER), lane // LAYER % FACE_CAP, lane % LAYER
    home = lax.rem(me + 1 + lax.broadcasted_iota(jnp.int32, shape, 0), ranges)
    layers = [layer_voxel(k, place) for k in range(6)]
    seen = jnp.zeros(shape, jnp.int32)
    ask = jnp.full(shape, -1, jnp.int32)
    for b in range(own_blocks):
        for k in range(6):
            entry = jnp.full(shape, -1, jnp.int32)
            for j in range(chans):
                entry = jnp.where(device == j, nbr_ref[j * own_blocks + b, k], entry)
            start = entry - home * block_count
            hit = (start >= 0) & (start < block_count)
            ask = jnp.where(hit & (seen == slot), start * PIECE + layers[k], ask)
            seen = seen + jnp.where(hit, 1, 0)
    return ask


def row_table(nbr_ref, ranges, chans, me, mine):
    block_count = nbr_ref.shape[0]
    own_blocks = block_count // chans
    width = block_count * PIECE
    lane = lane_ids(128)
    w = lane % 8
    place = 4 * (lane // 8 % 4) + w // 2
    inside, sides, ends = [], [], []
    homes = []
    for b in range(own_blocks):
        inside.append(PIECE * (mine * own_blocks + b) + 4 * (lane // 8) + w // 2)
        side = jnp.full(lane.shape, -1, jnp.int32)
        end = jnp.full(lane.shape, -1, jnp.int32)
        for k in range(6):
            entry = nbr_ref[mine * own_blocks + b, k]
            home = jnp.where(entry >= 0, entry // block_count, -1)
            rank = jnp.int32(0)
            for other in homes:
                rank = rank + jnp.where(other == home, 1, 0)
            homes.append(home)
            near = jnp.where(home == me, 1, 0)
            off = lax.rem(home - me + ranges, ranges)
            far_first = width + (off - 1) * FACE_CAP * LAYER + rank * LAYER
            first = jnp.where(near == 1, (entry - me * block_count) * PIECE, far_first)
            first = jnp.where(home >= 0, first, -(2**20))
            here = place if k < 4 else lane // 8
            target = first + here + near * (layer_voxel(k, here) - here)
            if k < 4:
                side = jnp.where(lane // 32 == k, target, side)
            else:
                end = jnp.where(w == 7 * (k - 4), target, end)
        sides.append(side)
        ends.append(end)
    return inside, sides, ends


def one_hot(depth, target, first=0):
    shape = (depth, target.shape[1])
    lanes = lax.broadcasted_iota(jnp.int32, shape, 0) + first
    return jnp.where(lanes == target, 1.0, 0.0).astype(jnp.bfloat16)


def each(count, body):
    if count <= 4:
        for i in range(count):
            body(i)
    else:
        lax.fori_loop(0, count, lambda i, c: (body(i), c)[1], 0)


def kernel(
    ranges,
    chans,
    dest_ref,
    nbr_ref,
    bias_ref,
    parents_hbm,
    up_hbm,
    conv_hbm,
    out_ref,
    parents_ref,
    up_ref,
    conv_ref,
    moves,
    moved,
    asks,
    asked,
    held,
    faces_out,
    faces_in,
    far_ref,
    cube,
    cols,
    load_sem,
    ask_send,
    ask_recv,
    move_send,
    move_recv,
    held_send,
    held_recv,
    face_send,
    face_recv,
):
    me = lax.axis_index("morton")
    mine = lax.axis_index("chan")
    total = ranges * chans
    own_blocks = out_ref.shape[0]
    block_count = nbr_ref.shape[0]
    parent_count, depth = parents_ref.shape[0], parents_ref.shape[1]
    half = depth // 2
    width = held.shape[2]
    move_width = MOVE_CAP * PIECE

    parents_load = pltpu.make_async_copy(parents_hbm, parents_ref, load_sem.at[2])
    up_load = pltpu.make_async_copy(up_hbm, up_ref, load_sem.at[0])
    conv_load = pltpu.make_async_copy(conv_hbm, conv_ref, load_sem.at[1])
    parents_load.start()
    up_load.start()
    conv_load.start()

    def at(range_id, chan_id):
        return {"morton": range_id, "chan": chan_id}

    barrier = pltpu.get_barrier_semaphore()
    here = me * chans + mine

    def greet(i):
        other = lax.rem(here + i + 1, total)
        pl.semaphore_signal(
            barrier, inc=1, device_id=at(other // chans, lax.rem(other, chans)), device_id_type=MESH
        )

    each(total - 1, greet)

    request = request_table(nbr_ref, ranges, chans, me)
    for m in range(ranges - 1):
        asks[m] = request[m : m + 1]
    pick = pick_table(dest_ref, ranges, block_count, me)
    inside, sides, ends = row_table(nbr_ref, ranges, chans, me, mine)
    inner_rows = jnp.concatenate(inside, axis=1)
    outer_rows = jnp.concatenate(sides + ends, axis=1)

    parents_load.wait()
    gathered = jnp.zeros((depth, pick.shape[1]), jnp.float32)
    for p in range(parent_count):
        gathered = gathered + jnp.dot(
            parents_ref[p], one_hot(512, pick, 512 * p), preferred_element_type=jnp.float32
        )
    gathered = gathered.astype(jnp.bfloat16)
    moves[0] = gathered[:, width : width + move_width]
    moves[1] = gathered[:, width + move_width :]
    held[mine] = gathered[:, :width]
    faces_in[ranges - 1] = jnp.zeros(faces_in.shape[1:], jnp.bfloat16)

    pl.semaphore_wait(barrier, total - 1)

    def ask_copy(m, arrives):
        return pltpu.make_async_remote_copy(
            src_ref=asks.at[m],
            dst_ref=asked.at[arrives],
            send_sem=ask_send.at[m],
            recv_sem=ask_recv.at[arrives],
            device_id=at(lax.rem(me + m + 1, ranges), mine),
            device_id_type=MESH,
        )

    def move_copy(side, i, source):
        other = lax.rem(me + (1 if side == 0 else ranges - 1), ranges)
        return pltpu.make_async_remote_copy(
            src_ref=moves.at[side],
            dst_ref=moved.at[side, source],
            send_sem=move_send.at[side, i],
            recv_sem=move_recv.at[side, i],
            device_id=at(other, lax.rem(mine + i, chans)),
            device_id_type=MESH,
        )

    def held_copy(i, source):
        return pltpu.make_async_remote_copy(
            src_ref=held.at[source],
            dst_ref=held.at[source],
            send_sem=held_send.at[i],
            recv_sem=held_recv.at[i],
            device_id=at(me, lax.rem(mine + i + 1, chans)),
            device_id_type=MESH,
        )

    each(ranges - 1, lambda m: ask_copy(m, ranges - 2 - m).start())
    for i in range(chans):
        for side in range(2):
            move_copy(side, i, mine).start()
    each(chans - 1, lambda i: held_copy(i, mine).start())

    def add_moved(block, low, high):
        first = block[:, :move_width].astype(jnp.float32) + low.astype(jnp.float32)
        last = block[:, width - move_width :].astype(jnp.float32) + high.astype(jnp.float32)
        return jnp.concatenate(
            [
                first.astype(jnp.bfloat16),
                block[:, move_width : width - move_width],
                last.astype(jnp.bfloat16),
            ],
            axis=1,
        )

    for side in range(2):
        move_copy(side, 0, mine).wait_recv()
    own = add_moved(gathered[:, :width], moved[0, mine], moved[1, mine])

    def face_copy(m, j, arrives, source):
        return pltpu.make_async_remote_copy(
            src_ref=faces_out.at[m, j],
            dst_ref=faces_in.at[arrives, source],
            send_sem=face_send.at[m, j],
            recv_sem=face_recv.at[arrives, source],
            device_id=at(lax.rem(me + m + 1, ranges), j),
            device_id_type=MESH,
        )

    def answer(m):
        ask_copy(m, m).wait_recv()
        found = jnp.dot(own, one_hot(width, asked[m]), preferred_element_type=jnp.float32)
        for j in range(chans):
            part = found[:, PIECE * j : PIECE * (j + 1)]
            faces_out[m, j] = jnp.concatenate([part[:half], part[half:]], axis=1).astype(jnp.bfloat16)
            face_copy(m, j, ranges - 2 - m, mine).start()

    each(ranges - 1, answer)

    for i in range(1, chans):
        source = lax.rem(mine + chans - i, chans)
        for side in range(2):
            move_copy(side, i, source).wait_recv()
        held_copy(i - 1, source).wait_recv()
    near = add_moved(
        held[...].reshape(chans * depth, width),
        moved[0].reshape(chans * depth, move_width),
        moved[1].reshape(chans * depth, move_width),
    )

    count = own_blocks * 128
    z_at = lax.rem(lax.broadcasted_iota(jnp.int32, (128, 128), 0), 8)
    odd = lax.rem(lax.broadcasted_iota(jnp.int32, (count, 128), 0), 2) == 1
    outer_high = jnp.concatenate([odd, jnp.logical_not(odd)], axis=0)

    def lift(voxels, high):
        lifted = {}
        for ox in range(2):
            for oy in range(2):
                low_z = jnp.dot(voxels, up_ref[4 * ox + 2 * oy], preferred_element_type=jnp.float32)
                high_z = jnp.dot(voxels, up_ref[4 * ox + 2 * oy + 1], preferred_element_type=jnp.float32)
                lifted[ox, oy] = jnp.where(high, high_z, low_z)
        return lifted

    inner = jnp.dot(near, one_hot(width, inner_rows), preferred_element_type=jnp.float32)
    outer = jnp.dot(near, one_hot(width, outer_rows), preferred_element_type=jnp.float32)
    up_load.wait()
    inner_up = lift(inner.T.astype(jnp.bfloat16), odd)

    def face_wait(m):
        for j in range(chans):
            face_copy(m, j, m, j).wait_recv()

    each(ranges - 1, face_wait)

    def unpack(m):
        both = faces_in[m].astype(jnp.float32)
        part = jnp.concatenate([both[:, :, :PIECE], both[:, :, PIECE:]], axis=1)
        return part.reshape(chans * depth, PIECE)

    def widen(i):
        first = i * 2 * PIECE if isinstance(i, int) else pl.multiple_of(i * 2 * PIECE, 2 * PIECE)
        far_ref[:, pl.ds(first, 2 * PIECE)] = jnp.concatenate(
            [unpack(2 * i), unpack(2 * i + 1)], axis=1
        ).astype(jnp.bfloat16)

    each(ranges // 2, widen)
    outer = outer + jnp.dot(
        far_ref[...],
        one_hot(far_ref.shape[1], outer_rows, width),
        preferred_element_type=jnp.float32,
    )
    outer_up = lift(outer.T.astype(jnp.bfloat16), outer_high)

    nothing = jnp.zeros((8, 128), jnp.float32)

    def shifts(middle, end):
        below = jnp.where(z_at == 0, end, pltpu.roll(middle, 1, 0))
        above = jnp.where(z_at == 7, end, pltpu.roll(middle, 127, 0))
        return below, middle, above

    conv_load.wait()
    for b in range(own_blocks):
        first = 128 * b
        for ox in range(2):
            for oy in range(2):
                outside = outer_up[ox, oy]
                inner = shifts(
                    inner_up[ox, oy][first : first + 128], outside[count + first : count + first + 128]
                )
                sides = shifts(outside[first : first + 128], 0.0)
                for dz in range(3):
                    for p in range(4):
                        for q in range(4):
                            at_row = 8 * (4 * p + q)
                            cube[dz, 1 + 2 * p + ox, 1 + 2 * q + oy] = inner[dz][at_row : at_row + 8]
                    for t in range(4):
                        face_x, face_y = 1 - ox, 3 - oy
                        low = 32 * face_x + 8 * t
                        cube[dz, 9 * face_x, 1 + 2 * t + oy] = sides[dz][low : low + 8]
                        low = 32 * face_y + 8 * t
                        cube[dz, 1 + 2 * t + ox, 9 * (face_y - 2)] = sides[dz][low : low + 8]
        for dz in range(3):
            for x in (0, 9):
                for y in (0, 9):
                    cube[dz, x, y] = nothing
        for x in range(10):
            for dy in range(3):
                for dz in range(3):
                    lane = 128 * (3 * dy + dz)
                    cols[x, :, lane : lane + 128] = (
                        cube[dz, x, dy : dy + 8].reshape(64, 128).astype(jnp.bfloat16)
                    )
        total_sum = jnp.zeros((512, 128), jnp.float32) + bias_ref[...]
        for dx in range(3):
            total_sum = total_sum + jnp.dot(
                cols[dx : dx + 8].reshape(512, 1152),
                conv_ref[9 * dx : 9 * dx + 9].reshape(1152, 128),
                preferred_element_type=jnp.float32,
            )
        result = total_sum / (1.0 + jnp.exp(-total_sum))
        out_ref[b] = result.T.astype(jnp.bfloat16)

    def finish(m):
        ask_copy(m, m).wait_send()
        for j in range(chans):
            face_copy(m, j, m, j).wait_send()

    each(ranges - 1, finish)
    for i in range(chans):
        for side in range(2):
            move_copy(side, i, mine).wait_send()
        if i > 0:
            held_copy(i - 1, mine).wait_send()


def per_device(parents, up_weight, conv_weight, conv_bias, child_dest, face_nbr):
    ranges, chans = lax.axis_size("morton"), lax.axis_size("chan")
    block_count = face_nbr.shape[0]
    own_blocks = block_count // chans
    depth = parents.shape[1]
    width = block_count * PIECE
    vmem = pl.BlockSpec(memory_space=pltpu.VMEM)
    smem = pl.BlockSpec(memory_space=pltpu.SMEM)
    hbm = pl.BlockSpec(memory_space=pltpu.HBM)
    ask_shape = (ranges - 1, 1, chans * FACE_CAP * LAYER)
    bf16 = jnp.bfloat16
    dma = pltpu.SemaphoreType.DMA
    return pl.pallas_call(
        functools.partial(kernel, ranges, chans),
        out_shape=jax.ShapeDtypeStruct((own_blocks, 128, 512), bf16),
        in_specs=[smem] * 2 + [vmem] + [hbm] * 3,
        out_specs=vmem,
        scratch_shapes=[
            pltpu.VMEM(parents.shape, bf16),
            pltpu.VMEM(up_weight.shape, bf16),
            pltpu.VMEM(conv_weight.shape, bf16),
            pltpu.VMEM((2, depth, MOVE_CAP * PIECE), bf16),
            pltpu.VMEM((2, chans, depth, MOVE_CAP * PIECE), bf16),
            pltpu.VMEM(ask_shape, jnp.int32),
            pltpu.VMEM(ask_shape, jnp.int32),
            pltpu.VMEM((chans, depth, width), bf16),
            pltpu.VMEM((ranges - 1, chans, depth // 2, 2 * PIECE), bf16),
            pltpu.VMEM((ranges, chans, depth // 2, 2 * PIECE), bf16),
            pltpu.VMEM((chans * depth, ranges * PIECE), bf16),
            pltpu.VMEM((3, 10, 10, 8, 128), jnp.float32),
            pltpu.VMEM((10, 64, 1152), bf16),
            dma((3,)),
            dma((ranges - 1,)),
            dma((ranges - 1,)),
            dma((2, chans)),
            dma((2, chans)),
            dma((chans - 1,)),
            dma((chans - 1,)),
            dma((ranges - 1, chans)),
            dma((ranges - 1, chans)),
        ],
        compiler_params=pltpu.CompilerParams(
            collective_id=0, has_side_effects=True, vmem_limit_bytes=56 * 1024 * 1024
        ),
        name="sparse_level",
    )(child_dest, face_nbr, conv_bias.reshape(1, -1), parents, up_weight, conv_weight)


def solution(mesh):
    placed = (
        P(("groups", "morton"), "chan", None),
        P(),
        P(),
        P(),
        P(("groups", "morton")),
        P(("groups", "morton"), None),
    )
    return jax.shard_map(
        per_device,
        mesh=mesh,
        in_specs=placed,
        out_specs=P(("groups", "morton", "chan"), None, None),
        check_vma=False,
    )
```

time: 29.9 us -> 21.4 us (0.72)
  local copies, waits for them, and re-layouts: 6.91 us -> 1.67 us
  other arithmetic: 4.34 us -> 0 us
  Pallas kernels: 18.1 us -> 19.5 us
    unnamed x28 -> x1, local copies, waits for them, and re-layouts: 3.95 us -> 1.67 us
    reduce_sum x3 -> x0, other arithmetic: 1.43 us -> none  [the longest x1 0.84 us: tables(): found = jnp.sum(jnp.where(match, cand_lane[None, :] + 1, 0), axis=1) - 1]
    pallas_call x1, Pallas kernels: 18.1 us -> 19.5 us  [per_device(): pl.pallas_call(functools.partial(kernel, ranges, chans), out_shape=jax.Sh...]
    broadcast_in_dim x15 -> x0, local copies, waits for them, and re-layouts: 0.94 us -> none  [the longest x4 0.27 us: tables(): jnp.where(jnp.asarray(w == 0), ends[:, 0, :, None], jnp.where(jnp.asarray...]
    reshape x3 -> x0, local copies, waits for them, and re-layouts: 0.93 us -> none  [the longest x1 0.77 us: tables(): entries = face_nbr.reshape(chans, own_blocks * 6)]
    select_n x6 -> x0, other arithmetic: 0.86 us -> none  [the longest x1 0.67 us: tables(): jnp.where(o_off[:, :4, None] >= 0, sides, -1).reshape(own_blocks, 128)]
    add x4 -> x0, other arithmetic: 0.85 us -> none  [the longest x1 0.77 us: tables(): value = start[:, None, :] + jnp.asarray(layer[face].T)[None] + 1]
    ge x4 -> x0, other arithmetic: 0.75 us -> none  [the longest x1 0.66 us: tables(): child_dest >= 0]
where the time goes in v2:
time: 21.4 us; the launch traced here: 21.2 us
  Pallas kernels  19.5 us (91%)
  local copies, waits for them, and re-layouts  1.67 us (8%)
    pallas_call x1, Pallas kernels, per_device(): pl.pallas_call(functools.partial(kernel, ranges, chans), out_shape=jax.Sh...  19.5 us
    unnamed x1, local copies, waits for them, and re-layouts  1.67 us

profile of v2, /device:TPU:0, one launch (start us, length us, event | category | flops | bytes accessed | tf_op | source)
XLA Modules:
  0.0 21.2 jit_solution(8905277294139056755)
XLA Ops:
  0.0 19.5 %sparse_level.1 = bf16[2,128,512]{2,1,0:T(8,128)(2,1)} custom-call(s32[16]{0:T(128)} %dest_ref.1, s32[8,6]{1,0:T(8,128)} %nbr_ref.1, f32[1,128]{1,0:T(1,128)} %bitcast.1, bf16[2,64,512]{2,1,0:T(8,128)(2,1)} %parents_hbm.1, bf16[8,256,128]{2,1,0:T(8,128)(2,1)} %up_hbm.1, bf16[27,128,128]{2,1,0:T(8,128)(2,1)} %conv_hbm.1), custom_call_target="tpu_custom_call" | custom-call | tf_op jit(solution)/shard_map/sparse_level/pallas_call | solution.py:409
  19.5 1.7 %copy.8 = bf16[2,128,512]{2,1,0:T(8,128)(2,1)} copy(bf16[2,128,512]{2,1,0:T(8,128)(2,1)} %sparse_level.1) | data formatting | bytes 524288

commit v3 on v2

--- a/solution.py
+++ b/solution.py
@@ -46,62 +46,66 @@
     return pick
 
 
-def request_table(nbr_ref, ranges, chans, me):
+def request_table(nbr_ref, ranges, me):
     block_count = nbr_ref.shape[0]
-    own_blocks = block_count // chans
-    shape = (ranges - 1, chans * FACE_CAP * LAYER)
+    shape = (ranges - 1, 2 * FACE_CAP * LAYER)
     lane = lane_ids(shape[1], shape[0])
-    device, slot, place = lane // (FACE_CAP * LAYER), lane // LAYER % FACE_CAP, lane % LAYER
+    slot, place = lane // LAYER, lane % LAYER
     home = lax.rem(me + 1 + lax.broadcasted_iota(jnp.int32, shape, 0), ranges)
     layers = [layer_voxel(k, place) for k in range(6)]
     seen = jnp.zeros(shape, jnp.int32)
     ask = jnp.full(shape, -1, jnp.int32)
-    for b in range(own_blocks):
+    for b in range(block_count):
         for k in range(6):
-            entry = jnp.full(shape, -1, jnp.int32)
-            for j in range(chans):
-                entry = jnp.where(device == j, nbr_ref[j * own_blocks + b, k], entry)
-            start = entry - home * block_count
+            start = nbr_ref[b, k] - home * block_count
             hit = (start >= 0) & (start < block_count)
             ask = jnp.where(hit & (seen == slot), start * PIECE + layers[k], ask)
             seen = seen + jnp.where(hit, 1, 0)
     return ask
 
 
-def row_table(nbr_ref, ranges, chans, me, mine):
+def inner_table(block_count, own_blocks, mine):
+    lane = lane_ids(128)
+    return jnp.concatenate(
+        [PIECE * (mine * own_blocks + b) + 4 * (lane // 8) + lane % 8 // 2 for b in range(own_blocks)],
+        axis=1,
+    )
+
+
+def outer_table(nbr_ref, ranges, own_blocks, me, mine):
     block_count = nbr_ref.shape[0]
-    own_blocks = block_count // chans
     width = block_count * PIECE
-    lane = lane_ids(128)
+    shape = (2 * own_blocks, 128)
+    lane = lane_ids(128, shape[0])
+    group = lax.broadcasted_iota(jnp.int32, shape, 0)
     w = lane % 8
-    place = 4 * (lane // 8 % 4) + w // 2
-    inside, sides, ends = [], [], []
-    homes = []
-    for b in range(own_blocks):
-        inside.append(PIECE * (mine * own_blocks + b) + 4 * (lane // 8) + w // 2)
-        side = jnp.full(lane.shape, -1, jnp.int32)
-        end = jnp.full(lane.shape, -1, jnp.int32)
+    end = group >= own_blocks
+    block = jnp.where(end, group - own_blocks, group)
+    face = jnp.where(end, jnp.where(w == 0, 4, jnp.where(w == 7, 5, 6)), lane // 32)
+    place = jnp.where(end, lane // 8, 4 * (lane // 8 % 4) + w // 2)
+    order = (mine * own_blocks + block) * 6 + face
+    entry = jnp.full(shape, -1, jnp.int32)
+    layer = place
+    for k in range(6):
+        layer = jnp.where(face == k, layer_voxel(k, place), layer)
+        for b in range(own_blocks):
+            entry = jnp.where(
+                (block == b) & (face == k), nbr_ref[mine * own_blocks + b, k], entry
+            )
+    home = entry >> (block_count.bit_length() - 1)
+    rank = jnp.zeros(shape, jnp.int32)
+    for b in range(block_count):
         for k in range(6):
-            entry = nbr_ref[mine * own_blocks + b, k]
-            home = jnp.where(entry >= 0, entry // block_count, -1)
-            rank = jnp.int32(0)
-            for other in homes:
-                rank = rank + jnp.where(other == home, 1, 0)
-            homes.append(home)
-            near = jnp.where(home == me, 1, 0)
-            off = lax.rem(home - me + ranges, ranges)
-            far_first = width + (off - 1) * FACE_CAP * LAYER + rank * LAYER
-            first = jnp.where(near == 1, (entry - me * block_count) * PIECE, far_first)
-            first = jnp.where(home >= 0, first, -(2**20))
-            here = place if k < 4 else lane // 8
-            target = first + here + near * (layer_voxel(k, here) - here)
-            if k < 4:
-                side = jnp.where(lane // 32 == k, target, side)
-            else:
-                end = jnp.where(w == 7 * (k - 4), target, end)
-        sides.append(side)
-        ends.append(end)
-    return inside, sides, ends
+            other = nbr_ref[b, k] >> (block_count.bit_length() - 1)
+            rank = rank + jnp.where((home == other) & (order > 6 * b + k), 1, 0)
+    off = lax.rem(home - me + ranges, ranges)
+    target = jnp.where(
+        off == 0,
+        (entry - me * block_count) * PIECE + layer,
+        width + (off - 1) * FACE_CAP * LAYER + rank * LAYER + place,
+    )
+    target = jnp.where(entry >= 0, target, -1)
+    return jnp.concatenate([target[g : g + 1] for g in range(shape[0])], axis=1)
 
 
 def one_hot(depth, target, first=0):
@@ -131,6 +135,8 @@
     parents_ref,
     up_ref,
     conv_ref,
+    pick_inner,
+    pick_outer,
     moves,
     moved,
     asks,
@@ -150,6 +156,8 @@
     held_recv,
     face_send,
     face_recv,
+    pass_send,
+    pass_recv,
 ):
     me = lax.axis_index("morton")
     mine = lax.axis_index("chan")
@@ -182,25 +190,9 @@
 
     each(total - 1, greet)
 
-    request = request_table(nbr_ref, ranges, chans, me)
+    request = request_table(nbr_ref, ranges, me)
     for m in range(ranges - 1):
         asks[m] = request[m : m + 1]
-    pick = pick_table(dest_ref, ranges, block_count, me)
-    inside, sides, ends = row_table(nbr_ref, ranges, chans, me, mine)
-    inner_rows = jnp.concatenate(inside, axis=1)
-    outer_rows = jnp.concatenate(sides + ends, axis=1)
-
-    parents_load.wait()
-    gathered = jnp.zeros((depth, pick.shape[1]), jnp.float32)
-    for p in range(parent_count):
-        gathered = gathered + jnp.dot(
-            parents_ref[p], one_hot(512, pick, 512 * p), preferred_element_type=jnp.float32
-        )
-    gathered = gathered.astype(jnp.bfloat16)
-    moves[0] = gathered[:, width : width + move_width]
-    moves[1] = gathered[:, width + move_width :]
-    held[mine] = gathered[:, :width]
-    faces_in[ranges - 1] = jnp.zeros(faces_in.shape[1:], jnp.bfloat16)
 
     pl.semaphore_wait(barrier, total - 1)
 
@@ -236,10 +228,38 @@
         )
 
     each(ranges - 1, lambda m: ask_copy(m, ranges - 2 - m).start())
-    for i in range(chans):
-        for side in range(2):
-            move_copy(side, i, mine).start()
+
+    pick = pick_table(dest_ref, ranges, block_count, me)
+    parents_load.wait()
+    gathered = jnp.zeros((depth, pick.shape[1]), jnp.float32)
+    for p in range(parent_count):
+        gathered = gathered + jnp.dot(
+            parents_ref[p], one_hot(512, pick, 512 * p), preferred_element_type=jnp.float32
+        )
+    gathered = gathered.astype(jnp.bfloat16)
+    moves[0] = gathered[:, width : width + move_width]
+    moves[1] = gathered[:, width + move_width :]
+    held[mine] = gathered[:, :width]
+
+    gives = (me < ranges - 1, me > 0)
+    takes = (me > 0, me < ranges - 1)
+    for side in range(2):
+
+        @pl.when(gives[side])
+        def _():
+            for i in range(chans):
+                move_copy(side, i, mine).start()
+
+        @pl.when(jnp.logical_not(takes[side]))
+        def _():
+            moved[side] = jnp.zeros(moved.shape[1:], jnp.bfloat16)
+
     each(chans - 1, lambda i: held_copy(i, mine).start())
+
+    faces_in[ranges - 1] = jnp.zeros(faces_in.shape[1:], jnp.bfloat16)
+    outer_rows = outer_table(nbr_ref, ranges, own_blocks, me, mine)
+    pick_outer[...] = one_hot(pick_outer.shape[0], outer_rows)
+    pick_inner[...] = one_hot(width, inner_table(block_count, own_blocks, mine))
 
     def add_moved(block, low, high):
         first = block[:, :move_width].astype(jnp.float32) + low.astype(jnp.float32)
@@ -254,33 +274,51 @@
         )
 
     for side in range(2):
-        move_copy(side, 0, mine).wait_recv()
+
+        @pl.when(takes[side])
+        def _():
+            move_copy(side, 0, mine).wait_recv()
+
     own = add_moved(gathered[:, :width], moved[0, mine], moved[1, mine])
 
-    def face_copy(m, j, arrives, source):
+    def face_copy(m, arrives):
         return pltpu.make_async_remote_copy(
-            src_ref=faces_out.at[m, j],
-            dst_ref=faces_in.at[arrives, source],
-            send_sem=face_send.at[m, j],
-            recv_sem=face_recv.at[arrives, source],
-            device_id=at(lax.rem(me + m + 1, ranges), j),
+            src_ref=faces_out.at[m],
+            dst_ref=faces_in.at[arrives, mine],
+            send_sem=face_send.at[m],
+            recv_sem=face_recv.at[arrives],
+            device_id=at(lax.rem(me + m + 1, ranges), mine),
+            device_id_type=MESH,
+        )
+
+    def pass_copy(m, i, source):
+        return pltpu.make_async_remote_copy(
+            src_ref=faces_in.at[m, source],
+            dst_ref=faces_in.at[m, source],
+            send_sem=pass_send.at[m, i],
+            recv_sem=pass_recv.at[m, i],
+            device_id=at(me, lax.rem(mine + i + 1, chans)),
             device_id_type=MESH,
         )
 
     def answer(m):
         ask_copy(m, m).wait_recv()
         found = jnp.dot(own, one_hot(width, asked[m]), preferred_element_type=jnp.float32)
-        for j in range(chans):
-            part = found[:, PIECE * j : PIECE * (j + 1)]
-            faces_out[m, j] = jnp.concatenate([part[:half], part[half:]], axis=1).astype(jnp.bfloat16)
-            face_copy(m, j, ranges - 2 - m, mine).start()
+        faces_out[m] = jnp.concatenate([found[:half, :PIECE], found[half:, :PIECE]], axis=1).astype(
+            jnp.bfloat16
+        )
+        face_copy(m, ranges - 2 - m).start()
 
     each(ranges - 1, answer)
 
     for i in range(1, chans):
         source = lax.rem(mine + chans - i, chans)
         for side in range(2):
-            move_copy(side, i, source).wait_recv()
+
+            @pl.when(takes[side])
+            def _():
+                move_copy(side, i, source).wait_recv()
+
         held_copy(i - 1, source).wait_recv()
     near = add_moved(
         held[...].reshape(chans * depth, width),
@@ -302,14 +340,21 @@
                 lifted[ox, oy] = jnp.where(high, high_z, low_z)
         return lifted
 
-    inner = jnp.dot(near, one_hot(width, inner_rows), preferred_element_type=jnp.float32)
-    outer = jnp.dot(near, one_hot(width, outer_rows), preferred_element_type=jnp.float32)
+    inner = jnp.dot(near, pick_inner[...], preferred_element_type=jnp.float32)
+
+    def pass_on(m):
+        face_copy(m, m).wait_recv()
+        for i in range(chans - 1):
+            pass_copy(m, i, mine).start()
+
+    each(ranges - 1, pass_on)
+    outer = jnp.dot(near, pick_outer[:width], preferred_element_type=jnp.float32)
     up_load.wait()
     inner_up = lift(inner.T.astype(jnp.bfloat16), odd)
 
     def face_wait(m):
-        for j in range(chans):
-            face_copy(m, j, m, j).wait_recv()
+        for i in range(chans - 1):
+            pass_copy(m, i, lax.rem(mine + chans - 1 - i, chans)).wait_recv()
 
     each(ranges - 1, face_wait)
 
@@ -327,7 +372,7 @@
     each(ranges // 2, widen)
     outer = outer + jnp.dot(
         far_ref[...],
-        one_hot(far_ref.shape[1], outer_rows, width),
+        pick_outer[width:],
         preferred_element_type=jnp.float32,
     )
     outer_up = lift(outer.T.astype(jnp.bfloat16), outer_high)
@@ -378,18 +423,22 @@
                 conv_ref[9 * dx : 9 * dx + 9].reshape(1152, 128),
                 preferred_element_type=jnp.float32,
             )
-        result = total_sum / (1.0 + jnp.exp(-total_sum))
-        out_ref[b] = result.T.astype(jnp.bfloat16)
+        out_ref[b] = total_sum.T
 
     def finish(m):
         ask_copy(m, m).wait_send()
-        for j in range(chans):
-            face_copy(m, j, m, j).wait_send()
+        face_copy(m, m).wait_send()
+        for i in range(chans - 1):
+            pass_copy(m, i, mine).wait_send()
 
     each(ranges - 1, finish)
     for i in range(chans):
         for side in range(2):
-            move_copy(side, i, mine).wait_send()
+
+            @pl.when(gives[side])
+            def _():
+                move_copy(side, i, mine).wait_send()
+
         if i > 0:
             held_copy(i - 1, mine).wait_send()
 
@@ -403,24 +452,27 @@
     vmem = pl.BlockSpec(memory_space=pltpu.VMEM)
     smem = pl.BlockSpec(memory_space=pltpu.SMEM)
     hbm = pl.BlockSpec(memory_space=pltpu.HBM)
-    ask_shape = (ranges - 1, 1, chans * FACE_CAP * LAYER)
+    ask_shape = (ranges - 1, 1, 2 * FACE_CAP * LAYER)
+    far_width = ranges * FACE_CAP * LAYER
     bf16 = jnp.bfloat16
     dma = pltpu.SemaphoreType.DMA
-    return pl.pallas_call(
+    total = pl.pallas_call(
         functools.partial(kernel, ranges, chans),
-        out_shape=jax.ShapeDtypeStruct((own_blocks, 128, 512), bf16),
+        out_shape=jax.ShapeDtypeStruct((own_blocks, 128, 512), jnp.float32),
         in_specs=[smem] * 2 + [vmem] + [hbm] * 3,
         out_specs=vmem,
         scratch_shapes=[
             pltpu.VMEM(parents.shape, bf16),
             pltpu.VMEM(up_weight.shape, bf16),
             pltpu.VMEM(conv_weight.shape, bf16),
+            pltpu.VMEM((width, own_blocks * 128), bf16),
+            pltpu.VMEM((width + far_width, own_blocks * 256), bf16),
             pltpu.VMEM((2, depth, MOVE_CAP * PIECE), bf16),
             pltpu.VMEM((2, chans, depth, MOVE_CAP * PIECE), bf16),
             pltpu.VMEM(ask_shape, jnp.int32),
             pltpu.VMEM(ask_shape, jnp.int32),
             pltpu.VMEM((chans, depth, width), bf16),
-            pltpu.VMEM((ranges - 1, chans, depth // 2, 2 * PIECE), bf16),
+            pltpu.VMEM((ranges - 1, depth // 2, 2 * PIECE), bf16),
             pltpu.VMEM((ranges, chans, depth // 2, 2 * PIECE), bf16),
             pltpu.VMEM((chans * depth, ranges * PIECE), bf16),
             pltpu.VMEM((3, 10, 10, 8, 128), jnp.float32),
@@ -432,14 +484,17 @@
             dma((2, chans)),
             dma((chans - 1,)),
             dma((chans - 1,)),
-            dma((ranges - 1, chans)),
-            dma((ranges - 1, chans)),
+            dma((ranges - 1,)),
+            dma((ranges - 1,)),
+            dma((ranges - 1, chans - 1)),
+            dma((ranges - 1, chans - 1)),
         ],
         compiler_params=pltpu.CompilerParams(
             collective_id=0, has_side_effects=True, vmem_limit_bytes=56 * 1024 * 1024
         ),
         name="sparse_level",
     )(child_dest, face_nbr, conv_bias.reshape(1, -1), parents, up_weight, conv_weight)
+    return (total / (1.0 + jnp.exp(-total))).astype(bf16)
 
 
 def solution(mesh):

time: 21.4 us -> 23.1 us (1.079)
  other arithmetic: 0 us -> 1.89 us
  local copies, waits for them, and re-layouts: 1.67 us -> 0 us
  Pallas kernels: 19.5 us -> 21.1 us
    convert_element_type x0 -> x1, other arithmetic: none -> 1.89 us  [per_device(): return (total / (1.0 + jnp.exp(-total))).astype(bf16)]
    unnamed x1 -> x0, local copies, waits for them, and re-layouts: 1.67 us -> none
    pallas_call x1, Pallas kernels: 19.5 us -> 21.1 us  [per_device(): pl.pallas_call(functools.partial(kernel, ranges, chans), out_shape=jax.Sh...]
where the time goes in v3:
time: 23.1 us; the launch traced here: 23 us
  Pallas kernels  21.1 us (91%)
  other arithmetic  1.89 us (8%)
    pallas_call x1, Pallas kernels, per_device(): pl.pallas_call(functools.partial(kernel, ranges, chans), out_shape=jax.Sh...  21.1 us
    convert_element_type x1, other arithmetic, per_device(): return (total / (1.0 + jnp.exp(-total))).astype(bf16)  1.89 us

profile of v3, /device:TPU:0, one launch (start us, length us, event | category | flops | bytes accessed | tf_op | source)
XLA Modules:
  0.0 23.0 jit_solution(6093837513859166001)
XLA Ops:
  0.0 21.1 %sparse_level.1 = f32[2,128,512]{2,1,0:T(8,128)} custom-call(s32[16]{0:T(128)} %dest_ref.1, s32[8,6]{1,0:T(8,128)} %nbr_ref.1, f32[1,128]{1,0:T(1,128)} %bitcast.1, bf16[2,64,512]{2,1,0:T(8,128)(2,1)} %parents_hbm.1, bf16[8,256,128]{2,1,0:T(8,128)(2,1)} %up_hbm.1, bf16[27,128,128]{2,1,0:T(8,128)(2,1)} %conv_hbm.1), custom_call_target="tpu_custom_call" | custom-call | tf_op jit(solution)/shard_map/sparse_level/pallas_call | solution.py:459
  21.1 1.9 %divide_convert_fusion = bf16[2,128,512]{2,1,0:T(8,128)(2,1)} fusion(f32[2,128,512]{2,1,0:T(8,128)} %sparse_level.1), kind=kLoop, calls=%fused_computation | loop fusion | flops 524288 | bytes 786432 | tf_op jit(solution)/shard_map/convert_element_type | solution.py:497

commit v4 on v3

--- a/solution.py
+++ b/solution.py
@@ -156,8 +156,6 @@
     held_recv,
     face_send,
     face_recv,
-    pass_send,
-    pass_recv,
 ):
     me = lax.axis_index("morton")
     mine = lax.axis_index("chan")
@@ -193,6 +191,20 @@
     request = request_table(nbr_ref, ranges, me)
     for m in range(ranges - 1):
         asks[m] = request[m : m + 1]
+    pick = pick_table(dest_ref, ranges, block_count, me)
+
+    def gather(columns):
+        found = jnp.zeros((depth, columns.shape[1]), jnp.float32)
+        for p in range(parent_count):
+            found = found + jnp.dot(
+                parents_ref[p], one_hot(512, columns, 512 * p), preferred_element_type=jnp.float32
+            )
+        return found.astype(jnp.bfloat16)
+
+    parents_load.wait()
+    passed = gather(pick[:, width:])
+    moves[0] = passed[:, :move_width]
+    moves[1] = passed[:, move_width:]
 
     pl.semaphore_wait(barrier, total - 1)
 
@@ -229,18 +241,6 @@
 
     each(ranges - 1, lambda m: ask_copy(m, ranges - 2 - m).start())
 
-    pick = pick_table(dest_ref, ranges, block_count, me)
-    parents_load.wait()
-    gathered = jnp.zeros((depth, pick.shape[1]), jnp.float32)
-    for p in range(parent_count):
-        gathered = gathered + jnp.dot(
-            parents_ref[p], one_hot(512, pick, 512 * p), preferred_element_type=jnp.float32
-        )
-    gathered = gathered.astype(jnp.bfloat16)
-    moves[0] = gathered[:, width : width + move_width]
-    moves[1] = gathered[:, width + move_width :]
-    held[mine] = gathered[:, :width]
-
     gives = (me < ranges - 1, me > 0)
     takes = (me > 0, me < ranges - 1)
     for side in range(2):
@@ -254,6 +254,8 @@
         def _():
             moved[side] = jnp.zeros(moved.shape[1:], jnp.bfloat16)
 
+    gathered = gather(pick[:, :width])
+    held[mine] = gathered
     each(chans - 1, lambda i: held_copy(i, mine).start())
 
     faces_in[ranges - 1] = jnp.zeros(faces_in.shape[1:], jnp.bfloat16)
@@ -279,37 +281,38 @@
         def _():
             move_copy(side, 0, mine).wait_recv()
 
-    own = add_moved(gathered[:, :width], moved[0, mine], moved[1, mine])
-
-    def face_copy(m, arrives):
+    own = add_moved(gathered, moved[0, mine], moved[1, mine])
+
+    def face_copy(m, i, arrives, source):
         return pltpu.make_async_remote_copy(
             src_ref=faces_out.at[m],
-            dst_ref=faces_in.at[arrives, mine],
-            send_sem=face_send.at[m],
-            recv_sem=face_recv.at[arrives],
-            device_id=at(lax.rem(me + m + 1, ranges), mine),
+            dst_ref=faces_in.at[arrives, source],
+            send_sem=face_send.at[m, i],
+            recv_sem=face_recv.at[arrives, i],
+            device_id=at(lax.rem(me + m + 1, ranges), lax.rem(mine + i, chans)),
             device_id_type=MESH,
         )
 
-    def pass_copy(m, i, source):
-        return pltpu.make_async_remote_copy(
-            src_ref=faces_in.at[m, source],
-            dst_ref=faces_in.at[m, source],
-            send_sem=pass_send.at[m, i],
-            recv_sem=pass_recv.at[m, i],
-            device_id=at(me, lax.rem(mine + i + 1, chans)),
-            device_id_type=MESH,
-        )
-
-    def answer(m):
-        ask_copy(m, m).wait_recv()
-        found = jnp.dot(own, one_hot(width, asked[m]), preferred_element_type=jnp.float32)
-        faces_out[m] = jnp.concatenate([found[:half, :PIECE], found[half:, :PIECE]], axis=1).astype(
-            jnp.bfloat16
-        )
-        face_copy(m, ranges - 2 - m).start()
-
-    each(ranges - 1, answer)
+    def answer(first, count):
+        ask = []
+        for m in range(count):
+            ask_copy(first + m, first + m).wait_recv()
+            ask.append(asked[first + m][:, :PIECE])
+        found = jnp.dot(
+            own, one_hot(width, jnp.concatenate(ask, axis=1)), preferred_element_type=jnp.float32
+        )
+        for m in range(count):
+            part = found[:, PIECE * m : PIECE * (m + 1)]
+            faces_out[first + m] = jnp.concatenate([part[:half], part[half:]], axis=1).astype(
+                jnp.bfloat16
+            )
+            for i in range(chans):
+                face_copy(first + m, i, ranges - 2 - first - m, mine).start()
+
+    if ranges <= 4:
+        answer(0, ranges - 1)
+    else:
+        each(ranges - 1, lambda m: answer(m, 1))
 
     for i in range(1, chans):
         source = lax.rem(mine + chans - i, chans)
@@ -342,19 +345,13 @@
 
     inner = jnp.dot(near, pick_inner[...], preferred_element_type=jnp.float32)
 
-    def pass_on(m):
-        face_copy(m, m).wait_recv()
-        for i in range(chans - 1):
-            pass_copy(m, i, mine).start()
-
-    each(ranges - 1, pass_on)
     outer = jnp.dot(near, pick_outer[:width], preferred_element_type=jnp.float32)
     up_load.wait()
     inner_up = lift(inner.T.astype(jnp.bfloat16), odd)
 
     def face_wait(m):
-        for i in range(chans - 1):
-            pass_copy(m, i, lax.rem(mine + chans - 1 - i, chans)).wait_recv()
+        for i in range(chans):
+            face_copy(m, i, m, lax.rem(mine + chans - i, chans)).wait_recv()
 
     each(ranges - 1, face_wait)
 
@@ -423,13 +420,13 @@
                 conv_ref[9 * dx : 9 * dx + 9].reshape(1152, 128),
                 preferred_element_type=jnp.float32,
             )
-        out_ref[b] = total_sum.T
+        result = total_sum / (1.0 + jnp.exp(-total_sum))
+        out_ref[b] = result.T.astype(jnp.bfloat16)
 
     def finish(m):
         ask_copy(m, m).wait_send()
-        face_copy(m, m).wait_send()
-        for i in range(chans - 1):
-            pass_copy(m, i, mine).wait_send()
+        for i in range(chans):
+            face_copy(m, i, m, mine).wait_send()
 
     each(ranges - 1, finish)
     for i in range(chans):
@@ -456,9 +453,9 @@
     far_width = ranges * FACE_CAP * LAYER
     bf16 = jnp.bfloat16
     dma = pltpu.SemaphoreType.DMA
-    total = pl.pallas_call(
+    return pl.pallas_call(
         functools.partial(kernel, ranges, chans),
-        out_shape=jax.ShapeDtypeStruct((own_blocks, 128, 512), jnp.float32),
+        out_shape=pltpu.VMEM((own_blocks, 128, 512), bf16),
         in_specs=[smem] * 2 + [vmem] + [hbm] * 3,
         out_specs=vmem,
         scratch_shapes=[
@@ -484,17 +481,14 @@
             dma((2, chans)),
             dma((chans - 1,)),
             dma((chans - 1,)),
-            dma((ranges - 1,)),
-            dma((ranges - 1,)),
-            dma((ranges - 1, chans - 1)),
-            dma((ranges - 1, chans - 1)),
+            dma((ranges - 1, chans)),
+            dma((ranges - 1, chans)),
         ],
         compiler_params=pltpu.CompilerParams(
             collective_id=0, has_side_effects=True, vmem_limit_bytes=56 * 1024 * 1024
         ),
         name="sparse_level",
     )(child_dest, face_nbr, conv_bias.reshape(1, -1), parents, up_weight, conv_weight)
-    return (total / (1.0 + jnp.exp(-total))).astype(bf16)
 
 
 def solution(mesh):

time: 23.1 us -> 19.2 us (0.83)
  Pallas kernels: 21.1 us -> 18.3 us
  other arithmetic: 1.89 us -> 0 us
  local copies, waits for them, and re-layouts: 0 us -> 0.71 us
    pallas_call x1, Pallas kernels: 21.1 us -> 18.3 us  [per_device(): pl.pallas_call(functools.partial(kernel, ranges, chans), out_shape=pltpu....]
    convert_element_type x1 -> x0, other arithmetic: 1.89 us -> none  [per_device(): return (total / (1.0 + jnp.exp(-total))).astype(bf16)]
    unnamed x0 -> x1, local copies, waits for them, and re-layouts: none -> 0.71 us
where the time goes in v4:
time: 19.2 us; the launch traced here: 19.1 us
  Pallas kernels  18.3 us (95%)
  local copies, waits for them, and re-layouts  0.71 us (4%)
    pallas_call x1, Pallas kernels, per_device(): pl.pallas_call(functools.partial(kernel, ranges, chans), out_shape=pltpu....  18.3 us
    unnamed x1, local copies, waits for them, and re-layouts  0.71 us

profile of v4, /device:TPU:0, one launch (start us, length us, event | category | flops | bytes accessed | tf_op | source)
XLA Modules:
  0.0 19.1 jit_solution(12812204384638656035)
XLA Ops:
  0.0 18.3 %sparse_level.1 = bf16[2,128,512]{2,1,0:T(8,128)(2,1)S(1)} custom-call(s32[16]{0:T(128)} %dest_ref.1, s32[8,6]{1,0:T(8,128)} %nbr_ref.1, f32[1,128]{1,0:T(1,128)} %bitcast.1, bf16[2,64,512]{2,1,0:T(8,128)(2,1)} %parents_hbm.1, bf16[8,256,128]{2,1,0:T(8,128)(2,1)} %up_hbm.1, bf16[27,128,128]{2,1,0:T(8,128)(2,1)} %conv_hbm.1), custom_call_target="tpu_custom_call" | custom-call | tf_op jit(solution)/shard_map/sparse_level/pallas_call | solution.py:456
  18.4 0.7 %copy.8 = bf16[2,128,512]{2,1,0:T(8,128)(2,1)} copy(bf16[2,128,512]{2,1,0:T(8,128)(2,1)S(1)} %sparse_level.1) | data formatting | bytes 524288

commit v5 on v4

--- a/solution.py
+++ b/solution.py
@@ -135,6 +135,8 @@
     parents_ref,
     up_ref,
     conv_ref,
+    up_pairs,
+    conv_wide,
     pick_inner,
     pick_outer,
     moves,
@@ -263,6 +265,13 @@
     pick_outer[...] = one_hot(pick_outer.shape[0], outer_rows)
     pick_inner[...] = one_hot(width, inner_table(block_count, own_blocks, mine))
 
+    up_load.wait()
+    for o in range(8):
+        up_pairs[o // 2, :, 128 * (o % 2) : 128 * (o % 2 + 1)] = up_ref[o]
+    conv_load.wait()
+    for dx in range(3):
+        conv_wide[:, 128 * dx : 128 * (dx + 1)] = conv_ref[9 * dx : 9 * dx + 9].reshape(1152, 128)
+
     def add_moved(block, low, high):
         first = block[:, :move_width].astype(jnp.float32) + low.astype(jnp.float32)
         last = block[:, width - move_width :].astype(jnp.float32) + high.astype(jnp.float32)
@@ -338,15 +347,13 @@
         lifted = {}
         for ox in range(2):
             for oy in range(2):
-                low_z = jnp.dot(voxels, up_ref[4 * ox + 2 * oy], preferred_element_type=jnp.float32)
-                high_z = jnp.dot(voxels, up_ref[4 * ox + 2 * oy + 1], preferred_element_type=jnp.float32)
-                lifted[ox, oy] = jnp.where(high, high_z, low_z)
+                both = jnp.dot(voxels, up_pairs[2 * ox + oy], preferred_element_type=jnp.float32)
+                lifted[ox, oy] = jnp.where(high, both[:, 128:], both[:, :128])
         return lifted
 
     inner = jnp.dot(near, pick_inner[...], preferred_element_type=jnp.float32)
 
     outer = jnp.dot(near, pick_outer[:width], preferred_element_type=jnp.float32)
-    up_load.wait()
     inner_up = lift(inner.T.astype(jnp.bfloat16), odd)
 
     def face_wait(m):
@@ -381,7 +388,6 @@
         above = jnp.where(z_at == 7, end, pltpu.roll(middle, 127, 0))
         return below, middle, above
 
-    conv_load.wait()
     for b in range(own_blocks):
         first = 128 * b
         for ox in range(2):
@@ -413,13 +419,8 @@
                     cols[x, :, lane : lane + 128] = (
                         cube[dz, x, dy : dy + 8].reshape(64, 128).astype(jnp.bfloat16)
                     )
-        total_sum = jnp.zeros((512, 128), jnp.float32) + bias_ref[...]
-        for dx in range(3):
-            total_sum = total_sum + jnp.dot(
-                cols[dx : dx + 8].reshape(512, 1152),
-                conv_ref[9 * dx : 9 * dx + 9].reshape(1152, 128),
-                preferred_element_type=jnp.float32,
-            )
+        taps = jnp.dot(cols[...].reshape(640, 1152), conv_wide[...], preferred_element_type=jnp.float32)
+        total_sum = taps[:512, :128] + taps[64:576, 128:256] + taps[128:, 256:] + bias_ref[...]
         result = total_sum / (1.0 + jnp.exp(-total_sum))
         out_ref[b] = result.T.astype(jnp.bfloat16)
 
@@ -462,6 +463,8 @@
             pltpu.VMEM(parents.shape, bf16),
             pltpu.VMEM(up_weight.shape, bf16),
             pltpu.VMEM(conv_weight.shape, bf16),
+            pltpu.VMEM((4, 256, 256), bf16),
+            pltpu.VMEM((1152, 384), bf16),
             pltpu.VMEM((width, own_blocks * 128), bf16),
             pltpu.VMEM((width + far_width, own_blocks * 256), bf16),
             pltpu.VMEM((2, depth, MOVE_CAP * PIECE), bf16),

time: 19.2 us -> 18.8 us (0.979)
  Pallas kernels: 18.3 us -> 17.9 us
    pallas_call x1, Pallas kernels: 18.3 us -> 17.9 us  [per_device(): pl.pallas_call(functools.partial(kernel, ranges, chans), out_shape=pltpu....]
where the time goes in v5:
time: 18.8 us; the launch traced here: 18.6 us
  Pallas kernels  17.9 us (95%)
  local copies, waits for them, and re-layouts  0.71 us (4%)
    pallas_call x1, Pallas kernels, per_device(): pl.pallas_call(functools.partial(kernel, ranges, chans), out_shape=pltpu....  17.9 us
    unnamed x1, local copies, waits for them, and re-layouts  0.71 us

profile of v5, /device:TPU:0, one launch (start us, length us, event | category | flops | bytes accessed | tf_op | source)
XLA Modules:
  0.0 18.6 jit_solution(8235020604692306860)
XLA Ops:
  0.0 17.9 %sparse_level.1 = bf16[2,128,512]{2,1,0:T(8,128)(2,1)S(1)} custom-call(s32[16]{0:T(128)} %dest_ref.1, s32[8,6]{1,0:T(8,128)} %nbr_ref.1, f32[1,128]{1,0:T(1,128)} %bitcast.1, bf16[2,64,512]{2,1,0:T(8,128)(2,1)} %parents_hbm.1, bf16[8,256,128]{2,1,0:T(8,128)(2,1)} %up_hbm.1, bf16[27,128,128]{2,1,0:T(8,128)(2,1)} %conv_hbm.1), custom_call_target="tpu_custom_call" | custom-call | tf_op jit(solution)/shard_map/sparse_level/pallas_call | solution.py:457
  17.9 0.7 %copy.8 = bf16[2,128,512]{2,1,0:T(8,128)(2,1)} copy(bf16[2,128,512]{2,1,0:T(8,128)(2,1)S(1)} %sparse_level.1) | data formatting | bytes 524288

commit v6 on v5

--- a/solution.py
+++ b/solution.py
@@ -356,6 +356,19 @@
     outer = jnp.dot(near, pick_outer[:width], preferred_element_type=jnp.float32)
     inner_up = lift(inner.T.astype(jnp.bfloat16), odd)
 
+    nothing = jnp.zeros((8, 128), jnp.float32)
+    for b in range(own_blocks):
+        for dz in range(3):
+            for x in (0, 9):
+                for y in (0, 9):
+                    cube[b, dz, x, y] = nothing
+        for ox in range(2):
+            for oy in range(2):
+                for p in range(4):
+                    for q in range(4):
+                        at_row = 128 * b + 8 * (4 * p + q)
+                        cube[b, 1, 1 + 2 * p + ox, 1 + 2 * q + oy] = inner_up[ox, oy][at_row : at_row + 8]
+
     def face_wait(m):
         for i in range(chans):
             face_copy(m, i, m, lax.rem(mine + chans - i, chans)).wait_recv()
@@ -380,8 +393,6 @@
         preferred_element_type=jnp.float32,
     )
     outer_up = lift(outer.T.astype(jnp.bfloat16), outer_high)
-
-    nothing = jnp.zeros((8, 128), jnp.float32)
 
     def shifts(middle, end):
         below = jnp.where(z_at == 0, end, pltpu.roll(middle, 1, 0))
@@ -398,29 +409,29 @@
                 )
                 sides = shifts(outside[first : first + 128], 0.0)
                 for dz in range(3):
-                    for p in range(4):
+                    for p in range(4 if dz != 1 else 0):
                         for q in range(4):
                             at_row = 8 * (4 * p + q)
-                            cube[dz, 1 + 2 * p + ox, 1 + 2 * q + oy] = inner[dz][at_row : at_row + 8]
+                            cube[b, dz, 1 + 2 * p + ox, 1 + 2 * q + oy] = inner[dz][at_row : at_row + 8]
                     for t in range(4):
                         face_x, face_y = 1 - ox, 3 - oy
                         low = 32 * face_x + 8 * t
-                        cube[dz, 9 * face_x, 1 + 2 * t + oy] = sides[dz][low : low + 8]
+                        cube[b, dz, 9 * face_x, 1 + 2 * t + oy] = sides[dz][low : low + 8]
                         low = 32 * face_y + 8 * t
-                        cube[dz, 1 + 2 * t + ox, 9 * (face_y - 2)] = sides[dz][low : low + 8]
-        for dz in range(3):
-            for x in (0, 9):
-                for y in (0, 9):
-                    cube[dz, x, y] = nothing
+                        cube[b, dz, 1 + 2 * t + ox, 9 * (face_y - 2)] = sides[dz][low : low + 8]
         for x in range(10):
             for dy in range(3):
                 for dz in range(3):
                     lane = 128 * (3 * dy + dz)
-                    cols[x, :, lane : lane + 128] = (
-                        cube[dz, x, dy : dy + 8].reshape(64, 128).astype(jnp.bfloat16)
+                    cols[b, x, :, lane : lane + 128] = (
+                        cube[b, dz, x, dy : dy + 8].reshape(64, 128).astype(jnp.bfloat16)
                     )
-        taps = jnp.dot(cols[...].reshape(640, 1152), conv_wide[...], preferred_element_type=jnp.float32)
-        total_sum = taps[:512, :128] + taps[64:576, 128:256] + taps[128:, 256:] + bias_ref[...]
+    taps = jnp.dot(
+        cols[...].reshape(own_blocks * 640, 1152), conv_wide[...], preferred_element_type=jnp.float32
+    )
+    for b in range(own_blocks):
+        rows = taps[640 * b : 640 * (b + 1)]
+        total_sum = rows[:512, :128] + rows[64:576, 128:256] + rows[128:, 256:] + bias_ref[...]
         result = total_sum / (1.0 + jnp.exp(-total_sum))
         out_ref[b] = result.T.astype(jnp.bfloat16)
 
@@ -475,8 +486,8 @@
             pltpu.VMEM((ranges - 1, depth // 2, 2 * PIECE), bf16),
             pltpu.VMEM((ranges, chans, depth // 2, 2 * PIECE), bf16),
             pltpu.VMEM((chans * depth, ranges * PIECE), bf16),
-            pltpu.VMEM((3, 10, 10, 8, 128), jnp.float32),
-            pltpu.VMEM((10, 64, 1152), bf16),
+            pltpu.VMEM((own_blocks, 3, 10, 10, 8, 128), jnp.float32),
+            pltpu.VMEM((own_blocks, 10, 64, 1152), bf16),
             dma((3,)),
             dma((ranges - 1,)),
             dma((ranges - 1,)),

time: 18.8 us -> 18.7 us (level)
  no operation moved by 1% of the time
where the time goes in v6:
time: 18.7 us; the launch traced here: 18.6 us
  Pallas kernels  17.9 us (96%)
  local copies, waits for them, and re-layouts  0.71 us (4%)
    pallas_call x1, Pallas kernels, per_device(): pl.pallas_call(functools.partial(kernel, ranges, chans), out_shape=pltpu....  17.9 us
    unnamed x1, local copies, waits for them, and re-layouts  0.71 us

profile of v6, /device:TPU:0, one launch (start us, length us, event | category | flops | bytes accessed | tf_op | source)
XLA Modules:
  0.0 18.6 jit_solution(6302998604982388408)
XLA Ops:
  0.0 17.9 %sparse_level.1 = bf16[2,128,512]{2,1,0:T(8,128)(2,1)S(1)} custom-call(s32[16]{0:T(128)} %dest_ref.1, s32[8,6]{1,0:T(8,128)} %nbr_ref.1, f32[1,128]{1,0:T(1,128)} %bitcast.1, bf16[2,64,512]{2,1,0:T(8,128)(2,1)} %parents_hbm.1, bf16[8,256,128]{2,1,0:T(8,128)(2,1)} %up_hbm.1, bf16[27,128,128]{2,1,0:T(8,128)(2,1)} %conv_hbm.1), custom_call_target="tpu_custom_call" | custom-call | tf_op jit(solution)/shard_map/sparse_level/pallas_call | solution.py:468
  17.9 0.7 %copy.8 = bf16[2,128,512]{2,1,0:T(8,128)(2,1)} copy(bf16[2,128,512]{2,1,0:T(8,128)(2,1)S(1)} %sparse_level.1) | data formatting | bytes 524288
